TPU v7x, 512 devices: a whole 4x4x16 slice. The times are simulated.
512 devices in a mesh: tm: 16 (over z), row: 4 (over y), col: 8 (over x, core).
Axes of the slice: x: 4, y: 4, z: 16, core: 2. Of those that a mesh axis runs over, the one named last changes fastest.
Arguments:
- features: bfloat16 [64, 32, 128, 192], P('tm', 'row', 'col'), may hold values from -6 to 6
- conv_first: bfloat16 [3, 3, 3, 192, 192], replicated, may hold values from -0.078125 to 0.078125
- conv_second: bfloat16 [3, 3, 3, 192, 192], replicated, may hold values from -0.078125 to 0.078125
- gain_first: float32 [192], replicated, may hold values from 0.25 to 1.75
- gain_second: float32 [192], replicated, may hold values from 0.25 to 1.75
Outputs:
- decoded: bfloat16 [64, 32, 128, 192], P('tm', 'row', 'col')
All inputs are finite; a program needn't handle non-finite values.
Results may differ from a plain program's by a relative error of at most 0.0043.
Values may be sent and summed in bfloat16 or wider, within the bound.
A program may use at most 128 MiB of HBM per device.

v0:
```python
import jax
import jax.numpy as jnp
from jax import lax
from jax.sharding import PartitionSpec as P


def shifted(value, axis, steps):
    count = lax.axis_size(axis)
    initial, last = (max(0, -steps), min(count, count - steps))
    return lax.ppermute(value, axis, [(source, source + steps) for source in range(initial, last)])


def extended_2(cells, sides, width):
    for axis, dim in sides:
        count = lax.axis_size(axis)
        ends = count - 1
        head = lax.slice_in_dim(cells, 0, width, axis=dim)
        tail = lax.slice_in_dim(cells, cells.shape[dim] - width, cells.shape[dim], axis=dim)
        cells = jnp.concatenate(
            [
                lax.ppermute(tail, axis, [(i, (i + 1) % count) for i in range(ends)]),
                cells,
                lax.ppermute(head, axis, [((i + 1) % count, i) for i in range(ends)]),
            ],
            axis=dim,
        )
    return cells


def norm_act(values, gain):
    mean_sq = jnp.mean(values * values, axis=-1, keepdims=True)
    return jax.nn.silu(values * lax.rsqrt(mean_sq + 1e-06) * gain)


def conv_valid(padded, weight):
    out_frames = padded.shape[0] - 2
    out_rows = padded.shape[1] - 2
    out_cols = padded.shape[2] - 2
    channels = padded.shape[3]
    stacked = weight.reshape(3, 9 * channels, weight.shape[4])
    summed = jnp.zeros((out_frames * out_rows * out_cols, weight.shape[4]), jnp.float32)
    for frame_tap in range(3):
        window = padded[frame_tap : frame_tap + out_frames]
        patches = jnp.concatenate(
            [
                window[:, row_tap : row_tap + out_rows, col_tap : col_tap + out_cols, :]
                for row_tap in range(3)
                for col_tap in range(3)
            ],
            axis=-1,
        )
        summed = summed + jnp.dot(
            patches.reshape(-1, 9 * channels),
            stacked[frame_tap],
            preferred_element_type=jnp.float32,
        )
    return summed.reshape(out_frames, out_rows, out_cols, weight.shape[4])


def shards(features, conv_first, conv_second, gain_first, gain_second):
    widened = features.astype(jnp.float32)
    hidden_first = norm_act(widened, gain_first).astype(jnp.bfloat16)
    earlier = shifted(hidden_first[-2:], "tm", 1)
    extended = jnp.concatenate([earlier, hidden_first], axis=0)
    padded = extended_2(extended, (("row", 1), ("col", 2)), 1)
    first_out = conv_valid(padded, conv_first)
    inner_act = norm_act(first_out, gain_second)
    hidden_second = inner_act.astype(jnp.bfloat16)
    prior = shifted(hidden_second[-2:], "tm", 1)
    hidden_second = jnp.concatenate([prior, hidden_second], axis=0)
    hidden_second = extended_2(hidden_second, (("row", 1), ("col", 2)), 1)
    second_out = conv_valid(hidden_second, conv_second)
    return (widened + second_out).astype(jnp.bfloat16)


def solution(mesh):
    in_specs = (P("tm", "row", "col", None), P(), P(), P(), P())
    out_specs = P("tm", "row", "col", None)
    return jax.shard_map(shards, mesh=mesh, in_specs=in_specs, out_specs=out_specs, check_vma=False)
```

profile of v0, /device:TPU:259, one launch (start us, length us, event | category | flops | bytes accessed | tf_op | source)
XLA Modules:
  0.0 92.1 jit_solution(5694755762725522614)
XLA Ops:
  2.3 2.6 %collective-permute-start = (bf16[2,8,16,192]{3,2,1,0:T(8,128)(2,1)S(1)}, bf16[2,8,16,192]{3,2,1,0:T(8,128)(2,1)S(1)}, u32[]{:S(2)}, u32[]{:S(2)}) collective-permute-start(bf16[2,8,16,192]{3,2,1,0:T(8,128)(2,1)S(1)} %slice.412), channel_id=1, source_target_pairs={{0,32},{32,64},{64,96},{96,128},{128,160},{160,192},{192,224},{224... | collective-permute-start | bytes 294920 | tf_op jit(solution)/shard_map/ppermute | solution.py:10
  5.0 3.2 %fusion.12 = (bf16[1,3,3,192,192]{4,3,2,1,0:T(8,128)(2,1)S(1)}, bf16[1,3,3,192,192]{4,3,2,1,0:T(8,128)(2,1)}, bf16[1,3,3,192,192]{4,3,2,1,0:T(8,128)(2,1)}) fusion(bf16[3,3,3,192,192]{4,3,2,1,0:T(8,128)(2,1)} %param.6), kind=kLoop, calls=%fused_computation.49 | loop fusion | bytes 3981312 | tf_op jit(solution)/shard_map/slice | solution.py:54
  8.1 1.6 %collective-permute-done = bf16[2,8,16,192]{3,2,1,0:T(8,128)(2,1)S(1)} collective-permute-done((bf16[2,8,16,192]{3,2,1,0:T(8,128)(2,1)S(1)}, bf16[2,8,16,192]{3,2,1,0:T(8,128)(2,1)S(1)}, u32[]{:S(2)}, u32[]{:S(2)}) %collective-permute-start) | collective-permute-done | bytes 98336 | tf_op jit(solution)/shard_map/ppermute | solution.py:10
  9.8 3.2 %collective-permute-start.1 = (bf16[6,1,16,192]{3,2,1,0:T(8,128)(2,1)S(1)}, bf16[6,1,16,192]{3,2,1,0:T(8,128)(2,1)S(1)}, u32[]{:S(2)}, u32[]{:S(2)}) collective-permute-start(bf16[6,1,16,192]{3,2,1,0:T(8,128)(2,1)S(1)} %get-tuple-element.77), channel_id=1, source_target_pairs={{0,8},{8,16},{16,24},{1,9},{9,17},{17,25},{2,10},{10,18},{18,26},{... | collective-permute-start | bytes 110600 | tf_op jit(solution)/shard_map/ppermute | solution.py:21
  13.0 1.3 %collective-permute-start.2 = (bf16[6,1,16,192]{3,2,1,0:T(8,128)(2,1)S(1)}, bf16[6,1,16,192]{3,2,1,0:T(8,128)(2,1)S(1)}, u32[]{:S(2)}, u32[]{:S(2)}) collective-permute-start(bf16[6,1,16,192]{3,2,1,0:T(8,128)(2,1)S(1)} %get-tuple-element.78), channel_id=1, source_target_pairs={{8,0},{16,8},{24,16},{9,1},{17,9},{25,17},{10,2},{18,10},{26,18},{... | collective-permute-start | bytes 110600 | tf_op jit(solution)/shard_map/ppermute | solution.py:23
  15.1 2.7 %collective-permute-done.2 = bf16[6,1,16,192]{3,2,1,0:T(8,128)(2,1)S(1)} collective-permute-done((bf16[6,1,16,192]{3,2,1,0:T(8,128)(2,1)S(1)}, bf16[6,1,16,192]{3,2,1,0:T(8,128)(2,1)S(1)}, u32[]{:S(2)}, u32[]{:S(2)}) %collective-permute-start.2) | collective-permute-done | bytes 36896 | tf_op jit(solution)/shard_map/ppermute | solution.py:23
  18.0 6.0 %collective-permute-start.3 = (bf16[6,10,1,192]{3,2,1,0:T(2,128)(2,1)S(1)}, bf16[6,10,1,192]{3,2,1,0:T(2,128)(2,1)S(1)}, u32[]{:S(2)}, u32[]{:S(2)}) collective-permute-start(bf16[6,10,1,192]{3,2,1,0:T(2,128)(2,1)S(1)} %get-tuple-element.54), channel_id=1, source_target_pairs={{0,1},{1,2},{2,3},{3,4},{4,5},{5,6},{6,7},{8,9},{9,10},{10,11},{11... | collective-permute-start | bytes 69128 | tf_op jit(solution)/shard_map/ppermute | solution.py:21
  24.0 1.9 %collective-permute-start.4 = (bf16[6,10,1,192]{3,2,1,0:T(2,128)(2,1)S(1)}, bf16[6,10,1,192]{3,2,1,0:T(2,128)(2,1)S(1)}, u32[]{:S(2)}, u32[]{:S(2)}) collective-permute-start(bf16[6,10,1,192]{3,2,1,0:T(2,128)(2,1)S(1)} %get-tuple-element.53), channel_id=1, source_target_pairs={{1,0},{2,1},{3,2},{4,3},{5,4},{6,5},{7,6},{9,8},{10,9},{11,10},{12... | collective-permute-start | bytes 69128 | tf_op jit(solution)/shard_map/ppermute | solution.py:23
  27.1 2.4 %collective-permute-done.4 = bf16[6,10,1,192]{3,2,1,0:T(2,128)(2,1)S(1)} collective-permute-done((bf16[6,10,1,192]{3,2,1,0:T(2,128)(2,1)S(1)}, bf16[6,10,1,192]{3,2,1,0:T(2,128)(2,1)S(1)}, u32[]{:S(2)}, u32[]{:S(2)}) %collective-permute-start.4) | collective-permute-done | bytes 23072 | tf_op jit(solution)/shard_map/ppermute | solution.py:23
  30.0 2.3 %fusion.15 = (bf16[4,8,16,192]{3,2,1,0:T(8,128)(2,1)}, bf16[4,8,16,192]{3,2,1,0:T(8,128)(2,1)}, bf16[4,8,16,192]{3,2,1,0:T(8,128)(2,1)}, bf16[4,8,16,192]{3,2,1,...) fusion(bf16[6,10,17,192]{3,2,1,0:T(8,128)(2,1)S(1)} %get-tuple-, ...), kind=kLoop, calls=%fused_computation.52 | loop fusion | bytes 7077888 | tf_op jit(solution)/shard_map/slice | solution.py:46
  32.3 2.7 %concatenate.102 = bf16[4,8,16,1728]{3,2,1,0:T(8,128)(2,1)S(1)} concatenate(bf16[4,8,16,192]{3,2,1,0:T(8,128)(2,1)} %get-tuple-element.81, bf16[4,8,16,192]{3,2,1,0:T(8,128)(2,1)} %get-tuple-element.90, bf16[4,8,16,192]{3,2,1,0:T(8,128)(2,1)} %get-tuple-element.37, bf16[4,8,16,192]{3,2,1,0:T(8,128)(2,1)} %get-tuple-element.82, bf16[4,8,16,192]{3,2,1,0:T(8,128)(2,1)S(1)} %get-tuple-element.74, ...), dimensions={3} | concatenate | bytes 3538944 | tf_op jit(solution)/shard_map/concatenate | solution.py:44
  35.0 1.9 %fusion.21 = f32[512,192]{0,1:T(8,128)S(1)} fusion(bf16[512,1728]{1,0:T(8,128)(2,1)S(1)} %bitcast.30, bf16[1728,192]{1,0:T(8,128)(2,1)} %bitcast.34), kind=kOutput, calls=%fused_computation.58 | convolution fusion | flops 339738624 | bytes 2826240 | tf_op jit(solution)/shard_map/dot_general | solution.py:52
  37.0 2.9 %concatenate.103 = bf16[4,8,16,1728]{3,2,1,0:T(8,128)(2,1)S(1)} concatenate(bf16[4,8,16,192]{3,2,1,0:T(8,128)(2,1)} %get-tuple-element.84, bf16[4,8,16,192]{3,2,1,0:T(8,128)(2,1)} %get-tuple-element.91, bf16[4,8,16,192]{3,2,1,0:T(8,128)(2,1)} %get-tuple-element.34, bf16[4,8,16,192]{3,2,1,0:T(8,128)(2,1)} %get-tuple-element.85, bf16[4,8,16,192]{3,2,1,0:T(8,128)(2,1)} %get-tuple-element.73, ...), dimensions={3} | concatenate | bytes 3538944 | tf_op jit(solution)/shard_map/concatenate | solution.py:44
  39.8 2.7 %convolution_add_fusion.3 = f32[512,192]{0,1:T(8,128)} fusion(f32[512,192]{0,1:T(8,128)S(1)} %fusion.21, bf16[512,1728]{1,0:T(8,128)(2,1)S(1)} %bitcast.28, bf16[1728,192]{1,0:T(8,128)(2,1)} %bitcast.37), kind=kOutput, calls=%fused_computation.3 | convolution fusion | flops 339836928 | bytes 3219456 | tf_op jit(solution)/shard_map/dot_general | solution.py:52
  42.5 2.8 %concatenate.104 = bf16[4,8,16,1728]{3,2,1,0:T(8,128)(2,1)S(1)} concatenate(bf16[4,8,16,192]{3,2,1,0:T(8,128)(2,1)} %get-tuple-element.87, bf16[4,8,16,192]{3,2,1,0:T(8,128)(2,1)} %get-tuple-element.92, bf16[4,8,16,192]{3,2,1,0:T(8,128)(2,1)} %get-tuple-element.31, bf16[4,8,16,192]{3,2,1,0:T(8,128)(2,1)} %get-tuple-element.88, bf16[4,8,16,192]{3,2,1,0:T(8,128)(2,1)S(1)} %fusion.7, ...), dimensions={3} | concatenate | bytes 3538944 | tf_op jit(solution)/shard_map/concatenate | solution.py:44
  45.3 1.8 %multiply_reduce_fusion = (f32[512]{0:T(512)S(1)}, f32[512,192]{0,1:T(8,128)S(1)}) fusion(f32[512,192]{0,1:T(8,128)} %convolution_add_fusion.3, bf16[512,1728]{1,0:T(8,128)(2,1)S(1)} %bitcast.26, bf16[1728,192]{1,0:T(8,128)(2,1)S(1)} %bitcast.32), kind=kOutput, calls=%fused_computation.29 | convolution fusion | flops 340033024 | bytes 3221504 | tf_op jit(solution)/shard_map/dot_general | solution.py:52
  47.7 1.9 %collective-permute-start.5 = (bf16[2,8,16,192]{3,2,1,0:T(8,128)(2,1)S(1)}, bf16[2,8,16,192]{3,2,1,0:T(8,128)(2,1)S(1)}, u32[]{:S(2)}, u32[]{:S(2)}) collective-permute-start(bf16[2,8,16,192]{3,2,1,0:T(8,128)(2,1)S(1)} %slice.439), channel_id=1, source_target_pairs={{0,32},{32,64},{64,96},{96,128},{128,160},{160,192},{192,224},{224... | collective-permute-start | bytes 294920 | tf_op jit(solution)/shard_map/ppermute | solution.py:10
  49.6 3.2 %fusion.11 = (bf16[1,3,3,192,192]{4,3,2,1,0:T(8,128)(2,1)}, bf16[1,3,3,192,192]{4,3,2,1,0:T(8,128)(2,1)S(1)}, bf16[1,3,3,192,192]{4,3,2,1,0:T(8,128)(2,1)}) fusion(bf16[3,3,3,192,192]{4,3,2,1,0:T(8,128)(2,1)} %param.7), kind=kLoop, calls=%fused_computation.48 | loop fusion | bytes 3981312 | tf_op jit(solution)/shard_map/slice | solution.py:54
  52.8 2.5 %collective-permute-done.5 = bf16[2,8,16,192]{3,2,1,0:T(8,128)(2,1)S(1)} collective-permute-done((bf16[2,8,16,192]{3,2,1,0:T(8,128)(2,1)S(1)}, bf16[2,8,16,192]{3,2,1,0:T(8,128)(2,1)S(1)}, u32[]{:S(2)}, u32[]{:S(2)}) %collective-permute-start.5) | collective-permute-done | bytes 98336 | tf_op jit(solution)/shard_map/ppermute | solution.py:10
  55.3 3.2 %collective-permute-start.6 = (bf16[6,1,16,192]{3,2,1,0:T(8,128)(2,1)S(1)}, bf16[6,1,16,192]{3,2,1,0:T(8,128)(2,1)S(1)}, u32[]{:S(2)}, u32[]{:S(2)}) collective-permute-start(bf16[6,1,16,192]{3,2,1,0:T(8,128)(2,1)S(1)} %get-tuple-element.71), channel_id=1, source_target_pairs={{0,8},{8,16},{16,24},{1,9},{9,17},{17,25},{2,10},{10,18},{18,26},{... | collective-permute-start | bytes 110600 | tf_op jit(solution)/shard_map/ppermute | solution.py:21
  58.5 1.3 %collective-permute-start.7 = (bf16[6,1,16,192]{3,2,1,0:T(8,128)(2,1)S(1)}, bf16[6,1,16,192]{3,2,1,0:T(8,128)(2,1)S(1)}, u32[]{:S(2)}, u32[]{:S(2)}) collective-permute-start(bf16[6,1,16,192]{3,2,1,0:T(8,128)(2,1)S(1)} %get-tuple-element.72), channel_id=1, source_target_pairs={{8,0},{16,8},{24,16},{9,1},{17,9},{25,17},{10,2},{18,10},{26,18},{... | collective-permute-start | bytes 110600 | tf_op jit(solution)/shard_map/ppermute | solution.py:23
  60.6 2.8 %collective-permute-done.7 = bf16[6,1,16,192]{3,2,1,0:T(8,128)(2,1)S(1)} collective-permute-done((bf16[6,1,16,192]{3,2,1,0:T(8,128)(2,1)S(1)}, bf16[6,1,16,192]{3,2,1,0:T(8,128)(2,1)S(1)}, u32[]{:S(2)}, u32[]{:S(2)}) %collective-permute-start.7) | collective-permute-done | bytes 36896 | tf_op jit(solution)/shard_map/ppermute | solution.py:23
  64.6 4.8 %collective-permute-start.8 = (bf16[6,10,1,192]{3,2,1,0:T(2,128)(2,1)S(1)}, bf16[6,10,1,192]{3,2,1,0:T(2,128)(2,1)S(1)}, u32[]{:S(2)}, u32[]{:S(2)}) collective-permute-start(bf16[6,10,1,192]{3,2,1,0:T(2,128)(2,1)S(1)} %get-tuple-element.50), channel_id=1, source_target_pairs={{0,1},{1,2},{2,3},{3,4},{4,5},{5,6},{6,7},{8,9},{9,10},{10,11},{11... | collective-permute-start | bytes 69128 | tf_op jit(solution)/shard_map/ppermute | solution.py:21
  69.5 1.9 %collective-permute-start.9 = (bf16[6,10,1,192]{3,2,1,0:T(2,128)(2,1)S(1)}, bf16[6,10,1,192]{3,2,1,0:T(2,128)(2,1)S(1)}, u32[]{:S(2)}, u32[]{:S(2)}) collective-permute-start(bf16[6,10,1,192]{3,2,1,0:T(2,128)(2,1)S(1)} %get-tuple-element.49), channel_id=1, source_target_pairs={{1,0},{2,1},{3,2},{4,3},{5,4},{6,5},{7,6},{9,8},{10,9},{11,10},{12... | collective-permute-start | bytes 69128 | tf_op jit(solution)/shard_map/ppermute | solution.py:23
  72.3 2.7 %collective-permute-done.9 = bf16[6,10,1,192]{3,2,1,0:T(2,128)(2,1)S(1)} collective-permute-done((bf16[6,10,1,192]{3,2,1,0:T(2,128)(2,1)S(1)}, bf16[6,10,1,192]{3,2,1,0:T(2,128)(2,1)S(1)}, u32[]{:S(2)}, u32[]{:S(2)}) %collective-permute-start.9) | collective-permute-done | bytes 23072 | tf_op jit(solution)/shard_map/ppermute | solution.py:23
  75.5 1.6 %fusion.13 = (bf16[4,8,16,192]{3,2,1,0:T(8,128)(2,1)}, bf16[4,8,16,192]{3,2,1,0:T(8,128)(2,1)}, bf16[4,8,16,192]{3,2,1,0:T(8,128)(2,1)}, bf16[4,8,16,192]{3,2,1,...) fusion(bf16[6,10,17,192]{3,2,1,0:T(8,128)(2,1)S(1)} %get-tuple-, ...), kind=kLoop, calls=%fused_computation.50 | loop fusion | bytes 3538944 | tf_op jit(solution)/shard_map/slice | solution.py:46
  77.0 1.4 %fusion.14 = (bf16[4,8,16,192]{3,2,1,0:T(8,128)(2,1)}, bf16[4,8,16,192]{3,2,1,0:T(8,128)(2,1)}, bf16[4,8,16,192]{3,2,1,0:T(8,128)(2,1)}, bf16[4,8,16,192]{3,2,1,...) fusion(bf16[6,10,17,192]{3,2,1,0:T(8,128)(2,1)S(1)} %get-tuple-, ...), kind=kLoop, calls=%fused_computation.51 | loop fusion | bytes 3538944 | tf_op jit(solution)/shard_map/slice | solution.py:46
  78.5 2.7 %concatenate.111 = bf16[4,8,16,1728]{3,2,1,0:T(8,128)(2,1)S(1)} concatenate(bf16[4,8,16,192]{3,2,1,0:T(8,128)(2,1)} %get-tuple-element.28, bf16[4,8,16,192]{3,2,1,0:T(8,128)(2,1)} %get-tuple-element.60, bf16[4,8,16,192]{3,2,1,0:T(8,128)(2,1)} %get-tuple-element.19, bf16[4,8,16,192]{3,2,1,0:T(8,128)(2,1)} %get-tuple-element.27, bf16[4,8,16,192]{3,2,1,0:T(8,128)(2,1)S(1)} %get-tuple-element.68, ...), dimensions={3} | concatenate | bytes 3538944 | tf_op jit(solution)/shard_map/concatenate | solution.py:44
  82.0 2.9 %concatenate.112 = bf16[4,8,16,1728]{3,2,1,0:T(8,128)(2,1)S(1)} concatenate(bf16[4,8,16,192]{3,2,1,0:T(8,128)(2,1)} %get-tuple-element.25, bf16[4,8,16,192]{3,2,1,0:T(8,128)(2,1)} %get-tuple-element.59, bf16[4,8,16,192]{3,2,1,0:T(8,128)(2,1)} %get-tuple-element.16, bf16[4,8,16,192]{3,2,1,0:T(8,128)(2,1)} %get-tuple-element.24, bf16[4,8,16,192]{3,2,1,0:T(8,128)(2,1)} %get-tuple-element.67, ...), dimensions={3} | concatenate | bytes 3538944 | tf_op jit(solution)/shard_map/concatenate | solution.py:44
  84.9 1.5 %convolution_add_fusion.1 = f32[512,192]{0,1:T(8,128)} fusion(f32[512,192]{0,1:T(8,128)S(1)} %fusion.22, bf16[512,1728]{1,0:T(8,128)(2,1)S(1)} %bitcast.29, bf16[1728,192]{1,0:T(8,128)(2,1)S(1)} %bitcast.36), kind=kOutput, calls=%fused_computation.1 | convolution fusion | flops 339836928 | bytes 3219456 | tf_op jit(solution)/shard_map/dot_general | solution.py:52
  86.4 2.9 %concatenate.113 = bf16[4,8,16,1728]{3,2,1,0:T(8,128)(2,1)S(1)} concatenate(bf16[4,8,16,192]{3,2,1,0:T(8,128)(2,1)} %get-tuple-element.22, bf16[4,8,16,192]{3,2,1,0:T(8,128)(2,1)} %get-tuple-element.58, bf16[4,8,16,192]{3,2,1,0:T(8,128)(2,1)} %get-tuple-element.13, bf16[4,8,16,192]{3,2,1,0:T(8,128)(2,1)} %get-tuple-element.21, bf16[4,8,16,192]{3,2,1,0:T(8,128)(2,1)S(1)} %multiply_convert_fusion, ...), dimensions={3} | concatenate | bytes 3538944 | tf_op jit(solution)/shard_map/concatenate | solution.py:44
  89.3 1.8 %convolution_add_fusion = f32[512,192]{0,1:T(8,128)S(1)} fusion(f32[512,192]{0,1:T(8,128)} %convolution_add_fusion.1, bf16[512,1728]{1,0:T(8,128)(2,1)S(1)} %bitcast.27, bf16[1728,192]{1,0:T(8,128)(2,1)S(1)} %bitcast.35), kind=kOutput, calls=%fused_computation | convolution fusion | flops 339836928 | bytes 3219456 | tf_op jit(solution)/shard_map/dot_general | solution.py:52
  (37 shorter events, 10.6 us)
Async XLA Ops:
  2.3 7.5 %collective-permute-start = (bf16[2,8,16,192]{3,2,1,0:T(8,128)(2,1)S(1)}, bf16[2,8,16,192]{3,2,1,0:T(8,128)(2,1)S(1)}, u32[]{:S(2)}, u32[]{:S(2)}) collective-permute-start(bf16[2,8,16,192]{3,2,1,0:T(8,128)(2,1)S(1)} %slice.412), channel_id=1, source_target_pairs={{0,32},{32,64},{64,96},{96,128},{128,160},{160,192},{192,224},{224... | collective-permute-start | bytes 294920 | tf_op jit(solution)/shard_map/ppermute | solution.py:10
  9.8 5.3 %collective-permute-start.1 = (bf16[6,1,16,192]{3,2,1,0:T(8,128)(2,1)S(1)}, bf16[6,1,16,192]{3,2,1,0:T(8,128)(2,1)S(1)}, u32[]{:S(2)}, u32[]{:S(2)}) collective-permute-start(bf16[6,1,16,192]{3,2,1,0:T(8,128)(2,1)S(1)} %get-tuple-element.77), channel_id=1, source_target_pairs={{0,8},{8,16},{16,24},{1,9},{9,17},{17,25},{2,10},{10,18},{18,26},{... | collective-permute-start | bytes 110600 | tf_op jit(solution)/shard_map/ppermute | solution.py:21
  13.0 4.8 %collective-permute-start.2 = (bf16[6,1,16,192]{3,2,1,0:T(8,128)(2,1)S(1)}, bf16[6,1,16,192]{3,2,1,0:T(8,128)(2,1)S(1)}, u32[]{:S(2)}, u32[]{:S(2)}) collective-permute-start(bf16[6,1,16,192]{3,2,1,0:T(8,128)(2,1)S(1)} %get-tuple-element.78), channel_id=1, source_target_pairs={{8,0},{16,8},{24,16},{9,1},{17,9},{25,17},{10,2},{18,10},{26,18},{... | collective-permute-start | bytes 110600 | tf_op jit(solution)/shard_map/ppermute | solution.py:23
  18.0 9.2 %collective-permute-start.3 = (bf16[6,10,1,192]{3,2,1,0:T(2,128)(2,1)S(1)}, bf16[6,10,1,192]{3,2,1,0:T(2,128)(2,1)S(1)}, u32[]{:S(2)}, u32[]{:S(2)}) collective-permute-start(bf16[6,10,1,192]{3,2,1,0:T(2,128)(2,1)S(1)} %get-tuple-element.54), channel_id=1, source_target_pairs={{0,1},{1,2},{2,3},{3,4},{4,5},{5,6},{6,7},{8,9},{9,10},{10,11},{11... | collective-permute-start | bytes 69128 | tf_op jit(solution)/shard_map/ppermute | solution.py:21
  24.0 5.5 %collective-permute-start.4 = (bf16[6,10,1,192]{3,2,1,0:T(2,128)(2,1)S(1)}, bf16[6,10,1,192]{3,2,1,0:T(2,128)(2,1)S(1)}, u32[]{:S(2)}, u32[]{:S(2)}) collective-permute-start(bf16[6,10,1,192]{3,2,1,0:T(2,128)(2,1)S(1)} %get-tuple-element.53), channel_id=1, source_target_pairs={{1,0},{2,1},{3,2},{4,3},{5,4},{6,5},{7,6},{9,8},{10,9},{11,10},{12... | collective-permute-start | bytes 69128 | tf_op jit(solution)/shard_map/ppermute | solution.py:23
  45.3 2.1 %copy-start.3 = (f32[192]{0:T(256)S(1)}, f32[192]{0:T(256)}, u32[]{:S(2)}) copy-start(f32[192]{0:T(256)} %param.9) | copy-start | bytes 2308
  47.7 7.7 %collective-permute-start.5 = (bf16[2,8,16,192]{3,2,1,0:T(8,128)(2,1)S(1)}, bf16[2,8,16,192]{3,2,1,0:T(8,128)(2,1)S(1)}, u32[]{:S(2)}, u32[]{:S(2)}) collective-permute-start(bf16[2,8,16,192]{3,2,1,0:T(8,128)(2,1)S(1)} %slice.439), channel_id=1, source_target_pairs={{0,32},{32,64},{64,96},{96,128},{128,160},{160,192},{192,224},{224... | collective-permute-start | bytes 294920 | tf_op jit(solution)/shard_map/ppermute | solution.py:10
  55.3 5.3 %collective-permute-start.6 = (bf16[6,1,16,192]{3,2,1,0:T(8,128)(2,1)S(1)}, bf16[6,1,16,192]{3,2,1,0:T(8,128)(2,1)S(1)}, u32[]{:S(2)}, u32[]{:S(2)}) collective-permute-start(bf16[6,1,16,192]{3,2,1,0:T(8,128)(2,1)S(1)} %get-tuple-element.71), channel_id=1, source_target_pairs={{0,8},{8,16},{16,24},{1,9},{9,17},{17,25},{2,10},{10,18},{18,26},{... | collective-permute-start | bytes 110600 | tf_op jit(solution)/shard_map/ppermute | solution.py:21
  58.5 4.8 %collective-permute-start.7 = (bf16[6,1,16,192]{3,2,1,0:T(8,128)(2,1)S(1)}, bf16[6,1,16,192]{3,2,1,0:T(8,128)(2,1)S(1)}, u32[]{:S(2)}, u32[]{:S(2)}) collective-permute-start(bf16[6,1,16,192]{3,2,1,0:T(8,128)(2,1)S(1)} %get-tuple-element.72), channel_id=1, source_target_pairs={{8,0},{16,8},{24,16},{9,1},{17,9},{25,17},{10,2},{18,10},{26,18},{... | collective-permute-start | bytes 110600 | tf_op jit(solution)/shard_map/ppermute | solution.py:23
  64.6 7.7 %collective-permute-start.8 = (bf16[6,10,1,192]{3,2,1,0:T(2,128)(2,1)S(1)}, bf16[6,10,1,192]{3,2,1,0:T(2,128)(2,1)S(1)}, u32[]{:S(2)}, u32[]{:S(2)}) collective-permute-start(bf16[6,10,1,192]{3,2,1,0:T(2,128)(2,1)S(1)} %get-tuple-element.50), channel_id=1, source_target_pairs={{0,1},{1,2},{2,3},{3,4},{4,5},{5,6},{6,7},{8,9},{9,10},{10,11},{11... | collective-permute-start | bytes 69128 | tf_op jit(solution)/shard_map/ppermute | solution.py:21
  69.5 5.5 %collective-permute-start.9 = (bf16[6,10,1,192]{3,2,1,0:T(2,128)(2,1)S(1)}, bf16[6,10,1,192]{3,2,1,0:T(2,128)(2,1)S(1)}, u32[]{:S(2)}, u32[]{:S(2)}) collective-permute-start(bf16[6,10,1,192]{3,2,1,0:T(2,128)(2,1)S(1)} %get-tuple-element.49), channel_id=1, source_target_pairs={{1,0},{2,1},{3,2},{4,3},{5,4},{6,5},{7,6},{9,8},{10,9},{11,10},{12... | collective-permute-start | bytes 69128 | tf_op jit(solution)/shard_map/ppermute | solution.py:23
  81.9 3.0 %copy-start.1 = (bf16[1,3,3,192,192]{4,3,2,1,0:T(8,128)(2,1)S(1)}, bf16[1,3,3,192,192]{4,3,2,1,0:T(8,128)(2,1)}, u32[]{:S(2)}) copy-start(bf16[1,3,3,192,192]{4,3,2,1,0:T(8,128)(2,1)} %get-tuple-element.7) | copy-start | bytes 1990660
  86.4 2.9 %copy-start = (bf16[1,3,3,192,192]{4,3,2,1,0:T(8,128)(2,1)S(1)}, bf16[1,3,3,192,192]{4,3,2,1,0:T(8,128)(2,1)}, u32[]{:S(2)}) copy-start(bf16[1,3,3,192,192]{4,3,2,1,0:T(8,128)(2,1)} %get-tuple-element.5) | copy-start | bytes 1990660
  89.3 2.0 %copy-start.2 = (bf16[4,8,16,192]{3,2,1,0:T(8,128)(2,1)S(1)}, bf16[4,8,16,192]{3,2,1,0:T(8,128)(2,1)}, u32[]{:S(2)}) copy-start(bf16[4,8,16,192]{3,2,1,0:T(8,128)(2,1)} %param.5) | copy-start | bytes 589828
where the time goes:
time: 93.4 us; the launch traced here: 92.1 us
  local copies, waits for them, and re-layouts  32.1 us (34%)
  starting transfers between devices  28.2 us (30%)
  waiting for transfers between devices  14.7 us (16%)
  matrix products  10.4 us (11%)
  other arithmetic  6.39 us (7%)
    ppermute x4, starting transfers between devices, extended_2(): lax.ppermute(tail, axis, [(i, (i + 1) % count) for i in range(ends)])  17.2 us
    concatenate x6, local copies, waits for them, and re-layouts, conv_valid(): jnp.concatenate([window[:, row_tap:row_tap + out_rows, col_tap:col_tap +...  16.9 us
    ppermute x4, waiting for transfers between devices, extended_2(): lax.ppermute(head, axis, [((i + 1) % count, i) for i in range(ends)])  10.5 us
    dot_general x6, matrix products, conv_valid(): jnp.dot(patches.reshape(-1, 9 * channels), stacked[frame_tap], preferred_...  10.4 us
    slice x6, local copies, waits for them, and re-layouts, conv_valid(): window[:, row_tap:row_tap + out_rows, col_tap:col_tap + out_cols, :]  8.27 us
    ppermute x4, starting transfers between devices, extended_2(): lax.ppermute(head, axis, [((i + 1) % count, i) for i in range(ends)])  6.43 us
    slice x2, local copies, waits for them, and re-layouts, conv_valid(): stacked[frame_tap]  6.36 us
    ppermute x2, starting transfers between devices, shifted(): lax.ppermute(value, axis, [(source, source + steps) for source in range(i...  4.57 us
  transfers between devices with their start and end apart: 10, of which 6 were waited for; matrix products, arithmetic and copies ran while one was open for 11% of the time, Pallas kernels for 0%

commit v1 on v0

v1 whole, which is shorter than its diff:
```python
import functools

import jax
import jax.numpy as jnp
from jax import lax
from jax.experimental import pallas as pl
from jax.experimental.pallas import tpu as pltpu
from jax.sharding import PartitionSpec as P

MESH = pl.DeviceIdType.MESH
BF = jnp.bfloat16
F32 = jnp.float32
C = 192
LO = 128
FR, RO, CO = 4, 8, 16
PX = RO * CO
EF, ER, EC = 6, 10, 32
SIDES = ((-1, 0), (1, 0), (0, -1), (0, 1), (-1, -1), (-1, 1), (1, -1), (1, 1))
SPOT = ((0, 48), (48, 48), (96, 32), (128, 32), (160, 16), (176, 16), (192, 16), (208, 16))
RIM = 224
BODY = 3 * PX


def opposite(side):
    dr, dc = SIDES[side]
    return SIDES.index((-dr, -dc))


def at(frame, row, col):
    return (frame * ER + row) * EC + col


def norm_act(low, high, gain_low, gain_high):
    total = jnp.sum(low * low + 0.5 * (high * high), axis=-1, keepdims=True)
    scale = lax.rsqrt(total * (1.0 / C) + 1e-06)

    def silu(values, gain):
        half = 0.5 * (values * scale * gain)
        return half + half * jnp.tanh(half)

    return silu(low, gain_low), silu(high, gain_high)


def twice(high):
    return jnp.concatenate([high, high], axis=-1)


def first_half(shape):
    return lax.broadcasted_iota(jnp.int32, shape, len(shape) - 1) < 64


def swap(value):
    return pltpu.roll(value, 64, 1)


def kernel(sizes, x_hbm, w1_hbm, w2_hbm, g1_hbm, g2_hbm, out_hbm,
           x, gains, wlo, whi, wti, elo, ehi, taps, body_s, body_r, rim_s, rim_r, out,
           load_sem, gain_sem, w_sem, out_sem, body_ss, body_rs, rim_ss, rim_rs, fwd_ss, fwd_rs):
    n_tm, n_row, n_col = sizes
    tm, row, col = (lax.axis_index(name) for name in ("tm", "row", "col"))

    loads = [pltpu.make_async_copy(x_hbm, x, load_sem)]
    for k, g in enumerate((g1_hbm, g2_hbm)):
        loads.append(pltpu.make_async_copy(g, gains.at[k], gain_sem.at[k]))
    for load in loads:
        load.start()
    w_loads = []
    for k, w in enumerate((w1_hbm, w2_hbm)):
        group = [
            pltpu.make_async_copy(w.at[:, :, :, 0:128, :], wlo.at[k], w_sem.at[k, 0]),
            pltpu.make_async_copy(w.at[:, :, 0:2, 128:192, :], whi.at[k], w_sem.at[k, 1]),
            pltpu.make_async_copy(w.at[:, :, 2, 128:192, :], wti.at[k, :, 0:3], w_sem.at[k, 2]),
        ]
        for load in group:
            load.start()
        w_loads.append(group)

    def neighbour(dr, dc):
        return (tm, lax.rem(row + (dr + n_row), n_row), lax.rem(col + (dc + n_col), n_col))

    later = (lax.rem(tm + 1, n_tm), row, col)
    earlier = (lax.rem(tm + (n_tm - 1), n_tm), row, col)
    barrier = pltpu.get_barrier_semaphore()
    for dr, dc in SIDES:
        pl.semaphore_signal(barrier, inc=1, device_id=neighbour(dr, dc), device_id_type=MESH)
    pl.semaphore_signal(barrier, inc=1, device_id=earlier, device_id_type=MESH)

    wti[:, :, 3] = jnp.zeros((2, 3, 64, C), BF)

    keep = {
        -1: jnp.where(row > 0, 1.0, 0.0),
        1: jnp.where(row < n_row - 1, 1.0, 0.0),
        -2: jnp.where(col > 0, 1.0, 0.0),
        2: jnp.where(col < n_col - 1, 1.0, 0.0),
    }
    keep_tm = jnp.where(tm > 0, 1.0, 0.0)

    def side_keep(side):
        dr, dc = SIDES[side]
        value = 1.0
        if dr:
            value = value * keep[dr]
        if dc:
            value = value * keep[2 * dc]
        return value

    def put_body(k, frame, low, high):
        for r in range(RO):
            elo[k, pl.ds(at(frame, r + 1, 8), CO)] = low[r * CO:(r + 1) * CO]
            ehi[k, pl.ds(at(frame, r + 1, 8), CO)] = high[r * CO:(r + 1) * CO]

    def body_copy(k):
        return pltpu.make_async_remote_copy(
            src_ref=body_s.at[k], dst_ref=body_r.at[k], send_sem=body_ss.at[k], recv_sem=body_rs.at[k],
            device_id=later, device_id_type=MESH)

    def forward_copy(k):
        return pltpu.make_async_remote_copy(
            src_ref=rim_r.at[k, 2], dst_ref=rim_r.at[k, 0], send_sem=fwd_ss.at[k], recv_sem=fwd_rs.at[k],
            device_id=later, device_id_type=MESH)

    def rim_copy(k, pair, side):
        here, size = SPOT[side]
        there, _ = SPOT[opposite(side)]
        return pltpu.make_async_remote_copy(
            src_ref=rim_s.at[k, pair, pl.ds(here, size)], dst_ref=rim_r.at[k, pair + 1, pl.ds(there, size)],
            send_sem=rim_ss.at[k, pair, side], recv_sem=rim_rs.at[k, pair, opposite(side)],
            device_id=neighbour(*SIDES[side]), device_id_type=MESH)

    def rim_wait(k, pair):
        for side in range(8):
            rim_copy(k, pair, side).wait_recv()

    def send_body(k):
        low = [elo[k, pl.ds(at(f, r, 8), CO)] for f in (4, 5) for r in range(1, 9)]
        body_s[k, 0:256] = jnp.concatenate(low, axis=0).astype(BF)
        mask = first_half((CO, LO))
        high = [jnp.where(mask, ehi[k, pl.ds(at(4, r, 8), CO)], ehi[k, pl.ds(at(5, r, 8), CO)]) for r in range(1, 9)]
        body_s[k, 256:384] = jnp.concatenate(high, axis=0).astype(BF)
        body_copy(k).start()

    def send_rims(k, pair):
        f = 2 + 2 * pair
        mask = first_half((CO, LO))
        for side, (dr, dc) in enumerate(SIDES):
            spot, _ = SPOT[side]
            r = 1 if dr < 0 else RO
            c = 8 if dc < 0 else 23
            if dc == 0:
                low = jnp.concatenate([elo[k, pl.ds(at(f + i, r, 8), CO)] for i in range(2)], axis=0)
                high = jnp.where(mask, *[ehi[k, pl.ds(at(f + i, r, 8), CO)] for i in range(2)])
                rim_s[k, pair, spot:spot + 32] = low.astype(BF)
                rim_s[k, pair, spot + 32:spot + 48] = high.astype(BF)
            elif dr == 0:
                low = jnp.concatenate([elo[k, pl.ds(at(f + i, 1, c), RO, stride=EC)] for i in range(2)], axis=0)
                high = jnp.where(mask[:RO], *[ehi[k, pl.ds(at(f + i, 1, c), RO, stride=EC)] for i in range(2)])
                rim_s[k, pair, spot:spot + 16] = low.astype(BF)
                rim_s[k, pair, spot + 16:spot + 32] = jnp.concatenate([high, high], axis=0).astype(BF)
            else:
                lines = lax.broadcasted_iota(jnp.int32, (8, LO), 0)
                value = jnp.zeros((8, LO), F32)
                for i, (ref, frame) in enumerate(((elo, f), (elo, f + 1), (ehi, f), (ehi, f + 1))):
                    line = jnp.broadcast_to(ref[k, pl.ds(at(frame, r, c), 1)], (8, LO))
                    value = jnp.where(lines == i, line, value)
                rim_s[k, pair, spot:spot + 16] = jnp.concatenate([value, value], axis=0).astype(BF)
            rim_copy(k, pair, side).start()

    def put_rims(k, slot):
        f = 2 * slot
        mask = first_half((CO, LO))
        for side, (dr, dc) in enumerate(SIDES):
            spot, _ = SPOT[side]
            r = 0 if dr < 0 else RO + 1
            c = 7 if dc < 0 else 24
            factor = side_keep(side)
            if slot == 0:
                factor = factor * keep_tm
            if dc == 0:
                low = rim_r[k, slot, spot:spot + 32].astype(F32) * factor
                high = rim_r[k, slot, spot + 32:spot + 48].astype(F32) * factor
                other = swap(high)
                for i in range(2):
                    elo[k, pl.ds(at(f + i, r, 8), CO)] = low[i * CO:(i + 1) * CO]
                ehi[k, pl.ds(at(f, r, 8), CO)] = jnp.where(mask, high, other)
                ehi[k, pl.ds(at(f + 1, r, 8), CO)] = jnp.where(mask, other, high)
            elif dr == 0:
                low = rim_r[k, slot, spot:spot + 16].astype(F32) * factor
                high = rim_r[k, slot, spot + 16:spot + 32].astype(F32)[:RO] * factor
                other = swap(high)
                for i in range(2):
                    elo[k, pl.ds(at(f + i, 1, c), RO, stride=EC)] = low[i * RO:(i + 1) * RO]
                ehi[k, pl.ds(at(f, 1, c), RO, stride=EC)] = jnp.where(mask[:RO], high, other)
                ehi[k, pl.ds(at(f + 1, 1, c), RO, stride=EC)] = jnp.where(mask[:RO], other, high)
            else:
                value = rim_r[k, slot, spot:spot + 16].astype(F32)[:8] * factor
                for i in range(2):
                    elo[k, pl.ds(at(f + i, r, c), 1)] = value[i:i + 1]
                    ehi[k, pl.ds(at(f + i, r, c), 1)] = value[i + 2:i + 3]

    def put_earlier(k):
        mask = first_half((PX, LO))
        low = body_r[k, 0:256].astype(F32) * keep_tm
        high = body_r[k, 256:384].astype(F32) * keep_tm
        other = swap(high)
        put_body(k, 0, low[:PX], jnp.where(mask, high, other))
        put_body(k, 1, low[PX:], jnp.where(mask, other, high))

    def build(k, frame):
        mask = first_half((CO, LO))

        def line(r, _):
            low = [elo[k, pl.ds(at(frame, r, 7 + c), CO)] for c in range(3)]
            high = [ehi[k, pl.ds(at(frame, r, 7 + c), CO)] for c in range(3)]
            below = ehi[k, pl.ds(at(frame, min(r + 1, ER - 1), 9), CO)]
            lines = pl.ds(r * CO, CO)
            for c in range(3):
                taps[k, frame, lines, c * LO:(c + 1) * LO] = low[c].astype(BF)
            taps[k, frame, lines, 3 * LO:4 * LO] = jnp.where(mask, high[0], high[1]).astype(BF)
            taps[k, frame, lines, 4 * LO:5 * LO] = jnp.where(mask, high[2], below).astype(BF)

        for r in range(ER):
            line(r, None)

    def conv(k, frame):
        total = None
        for a in range(3):
            f = frame - 2 + a
            left = [taps[k, f:f + 2, b * CO:b * CO + PX, 0:4 * LO].reshape(2 * PX, 4 * LO) for b in range(3)]
            left += [taps[k, f:f + 2, b * CO:b * CO + PX, 4 * LO:5 * LO].reshape(2 * PX, LO) for b in (0, 2)]
            right = []
            for b in range(3):
                right += [wlo[k, a, b].reshape(3 * LO, C), whi[k, a, b].reshape(LO, C)]
            right.append(wti[k, a].reshape(2 * LO, C))
            part = jnp.dot(jnp.concatenate(left, axis=1), jnp.concatenate(right, axis=0), preferred_element_type=F32)
            total = part if total is None else total + part
        return total

    for load in loads:
        load.wait()
    gain = []
    for k in range(2):
        value = gains[k]
        gain.append((value[:, :LO], twice(value[:, LO:])))
    for f in (2, 3, 0, 1):
        value = x[f].reshape(PX, C).astype(F32)
        put_body(0, f + 2, *norm_act(value[:, :LO], twice(value[:, LO:]), *gain[0]))

    pl.semaphore_wait(barrier, 9)
    send_rims(0, 1)
    send_rims(0, 0)
    send_body(0)

    def finish_first(frame):
        total = conv(0, frame)
        low, high = norm_act(total[:, :LO], twice(total[:, LO:]), *gain[1])
        for i in range(2):
            put_body(1, frame + i, low[i * PX:(i + 1) * PX], high[i * PX:(i + 1) * PX])

    def finish_second(frame):
        f = frame - 2
        total = conv(1, frame) + x[f:f + 2].reshape(2 * PX, C).astype(F32)
        out[f:f + 2] = total.astype(BF).reshape(2, RO, CO, C)
        pltpu.make_async_copy(out.at[f:f + 2], out_hbm.at[f:f + 2], out_sem.at[f // 2]).start()

    rim_wait(0, 1)
    forward_copy(0).start()
    put_rims(0, 2)
    build(0, 4)
    build(0, 5)
    rim_wait(0, 0)
    put_rims(0, 1)
    build(0, 2)
    build(0, 3)
    for load in w_loads[0]:
        load.wait()
    finish_first(4)
    send_rims(1, 1)
    send_body(1)

    body_copy(0).wait_recv()
    forward_copy(0).wait_recv()
    put_earlier(0)
    put_rims(0, 0)
    build(0, 0)
    build(0, 1)
    finish_first(2)
    send_rims(1, 0)

    rim_wait(1, 1)
    forward_copy(1).start()
    put_rims(1, 2)
    build(1, 4)
    build(1, 5)
    rim_wait(1, 0)
    put_rims(1, 1)
    build(1, 2)
    build(1, 3)
    for load in w_loads[1]:
        load.wait()
    finish_second(4)

    body_copy(1).wait_recv()
    forward_copy(1).wait_recv()
    put_earlier(1)
    put_rims(1, 0)
    build(1, 0)
    build(1, 1)
    finish_second(2)

    for k in range(2):
        body_copy(k).wait_send()
        forward_copy(k).wait_send()
        for pair in range(2):
            for side in range(8):
                rim_copy(k, pair, side).wait_send()
    for f in (2, 0):
        pltpu.make_async_copy(out.at[f:f + 2], out_hbm.at[f:f + 2], out_sem.at[f // 2]).wait()


def solution(mesh):
    sizes = tuple(mesh.shape[name] for name in ("tm", "row", "col"))

    def shards(features, conv_first, conv_second, gain_first, gain_second):
        anywhere = pl.BlockSpec(memory_space=pl.ANY)
        dma = pltpu.SemaphoreType.DMA
        return pl.pallas_call(
            functools.partial(kernel, sizes),
            out_shape=jax.ShapeDtypeStruct(features.shape, BF),
            in_specs=[anywhere] * 5,
            out_specs=anywhere,
            scratch_shapes=[
                pltpu.VMEM((FR, RO, CO, C), BF),
                pltpu.VMEM((2, 1, C), F32),
                pltpu.VMEM((2, 3, 3, 3, LO, C), BF),
                pltpu.VMEM((2, 3, 3, 2, 64, C), BF),
                pltpu.VMEM((2, 3, 4, 64, C), BF),
                pltpu.VMEM((2, EF * ER * EC, LO), F32),
                pltpu.VMEM((2, EF * ER * EC, LO), F32),
                pltpu.VMEM((2, EF, ER * CO, 5 * LO), BF),
                pltpu.VMEM((2, BODY, LO), BF),
                pltpu.VMEM((2, BODY, LO), BF),
                pltpu.VMEM((2, 2, RIM, LO), BF),
                pltpu.VMEM((2, 3, RIM, LO), BF),
                pltpu.VMEM((FR, RO, CO, C), BF),
                dma, dma((2,)), dma((2, 3)), dma((2,)),
                dma((2,)), dma((2,)), dma((2, 2, 8)), dma((2, 2, 8)), dma((2,)), dma((2,)),
            ],
            compiler_params=pltpu.CompilerParams(
                collective_id=0, has_side_effects=True, vmem_limit_bytes=48 * 1024 * 1024),
        )(features, conv_first, conv_second, gain_first.reshape(1, C), gain_second.reshape(1, C))

    return jax.shard_map(
        shards, mesh=mesh, in_specs=(P("tm", "row", "col", None), P(), P(), P(), P()),
        out_specs=P("tm", "row", "col", None), check_vma=False)
```

time: 93.4 us -> 38.4 us (0.41)
  the two profiles are of different devices: /device:TPU:259 before, /device:TPU:1 now
where the time goes in v1:
time: 38.4 us; the launch traced here: 38.2 us
  Pallas kernels  31.6 us (82%)
  local copies, waits for them, and re-layouts  6.51 us (17%)
    pallas_call x1, Pallas kernels, shards(): pl.pallas_call(functools.partial(kernel, sizes), out_shape=jax.ShapeDtype...  31.6 us
    unnamed x11, local copies, waits for them, and re-layouts  6.51 us

profile of v1, /device:TPU:1, one launch (start us, length us, event | category | flops | bytes accessed | tf_op | source)
XLA Modules:
  0.0 38.2 jit_solution(14420784962690965443)
XLA Ops:
  0.0 0.0 copy-start
  0.0 1.7 %copy-done = bf16[3,3,3,192,192]{4,3,2,1,0:T(8,128)(2,1)S(1)} copy-done((bf16[3,3,3,192,192]{4,3,2,1,0:T(8,128)(2,1)S(1)}, bf16[3,3,3,192,192]{4,3,2,1,0:T(8,128)(2,1)}, u32[]{:S(2)}) %copy-start) | copy-done | bytes 1990680
  1.8 0.0 copy-start.1
  1.8 1.7 %copy-done.1 = bf16[3,3,3,192,192]{4,3,2,1,0:T(8,128)(2,1)S(1)} copy-done((bf16[3,3,3,192,192]{4,3,2,1,0:T(8,128)(2,1)S(1)}, bf16[3,3,3,192,192]{4,3,2,1,0:T(8,128)(2,1)}, u32[]{:S(2)}) %copy-start.1) | copy-done | bytes 1990680
  3.5 0.0 copy-start.2
  3.5 0.9 %copy-done.2 = bf16[4,8,16,192]{3,2,1,0:T(8,128)(2,1)S(1)} copy-done((bf16[4,8,16,192]{3,2,1,0:T(8,128)(2,1)S(1)}, bf16[4,8,16,192]{3,2,1,0:T(8,128)(2,1)}, u32[]{:S(2)}) %copy-start.2) | copy-done | bytes 196632
  4.5 0.0 copy-start.3
  4.5 0.7 %copy-done.3 = f32[192]{0:T(256)S(1)} copy-done((f32[192]{0:T(256)S(1)}, f32[192]{0:T(256)}, u32[]{:S(2)}) %copy-start.3) | copy-done | bytes 792
  5.1 0.0 copy-start.4
  5.1 0.7 %copy-done.4 = f32[192]{0:T(256)S(1)} copy-done((f32[192]{0:T(256)S(1)}, f32[192]{0:T(256)}, u32[]{:S(2)}) %copy-start.4) | copy-done | bytes 792
  5.8 31.6 %shard_map.55 = bf16[4,8,16,192]{3,2,1,0:T(8,128)(2,1)S(1)} custom-call(bf16[4,8,16,192]{3,2,1,0:T(8,128)(2,1)S(1)} %copy-done.2, bf16[3,3,3,192,192]{4,3,2,1,0:T(8,128)(2,1)S(1)} %copy-done, bf16[3,3,3,192,192]{4,3,2,1,0:T(8,128)(2,1)S(1)} %copy-done.1, f32[1,192]{1,0:T(1,128)S(1)} %bitcast.2, f32[1,192]{1,0:T(1,128)S(1)} %bitcast.3), custom_call_target="tpu_custom_call" | custom-call | tf_op jit(solution)/shard_map/pallas_call | solution.py:326
  37.5 0.7 %copy.7 = bf16[4,8,16,192]{3,2,1,0:T(8,128)(2,1)} copy(bf16[4,8,16,192]{3,2,1,0:T(8,128)(2,1)S(1)} %shard_map.55) | data formatting | bytes 393216
Async XLA Ops:
  0.0 1.7 %copy-start = (bf16[3,3,3,192,192]{4,3,2,1,0:T(8,128)(2,1)S(1)}, bf16[3,3,3,192,192]{4,3,2,1,0:T(8,128)(2,1)}, u32[]{:S(2)}) copy-start(bf16[3,3,3,192,192]{4,3,2,1,0:T(8,128)(2,1)} %w1_hbm.1) | copy-start | bytes 5971972
  1.8 1.7 %copy-start.1 = (bf16[3,3,3,192,192]{4,3,2,1,0:T(8,128)(2,1)S(1)}, bf16[3,3,3,192,192]{4,3,2,1,0:T(8,128)(2,1)}, u32[]{:S(2)}) copy-start(bf16[3,3,3,192,192]{4,3,2,1,0:T(8,128)(2,1)} %w2_hbm.1) | copy-start | bytes 5971972
  3.5 0.9 %copy-start.2 = (bf16[4,8,16,192]{3,2,1,0:T(8,128)(2,1)S(1)}, bf16[4,8,16,192]{3,2,1,0:T(8,128)(2,1)}, u32[]{:S(2)}) copy-start(bf16[4,8,16,192]{3,2,1,0:T(8,128)(2,1)} %x_hbm.1) | copy-start | bytes 589828
  4.5 0.7 %copy-start.3 = (f32[192]{0:T(256)S(1)}, f32[192]{0:T(256)}, u32[]{:S(2)}) copy-start(f32[192]{0:T(256)} %param.8) | copy-start | bytes 2308
  5.1 0.7 %copy-start.4 = (f32[192]{0:T(256)S(1)}, f32[192]{0:T(256)}, u32[]{:S(2)}) copy-start(f32[192]{0:T(256)} %param.9) | copy-start | bytes 2308

commit v2 on v0

v2 whole, which is shorter than its diff:
```python
import functools

import jax
import jax.numpy as jnp
from jax import lax
from jax.experimental import pallas as pl
from jax.experimental.pallas import tpu as pltpu
from jax.sharding import PartitionSpec as P

MESH = pl.DeviceIdType.MESH
BF = jnp.bfloat16
F32 = jnp.float32
C = 192
LO = 128
FR, RO, CO = 4, 8, 16
PX = RO * CO
EF, ER1, ER2, EC = 6, 12, 10, 32
MAIN, SIDE = ER2 * CO, 2 * CO
SIDES = ((-1, 0), (1, 0), (0, -1), (0, 1), (-1, -1), (-1, 1), (1, -1), (1, 1))
SPOT = ((0, 96), (96, 96), (192, 48), (240, 48), (288, 16), (304, 16), (320, 16), (336, 16))
RIM = 352
BODY = 3 * PX
LATE = 3 * (MAIN + SIDE)


def opposite(side):
    dr, dc = SIDES[side]
    return SIDES.index((-dr, -dc))


def at1(frame, row, col):
    return (frame * ER1 + row) * EC + col


def at2(frame, row, col):
    return (frame * ER2 + row) * EC + col


def norm_act(low, high, gain_low, gain_high):
    total = jnp.sum(low * low + 0.5 * (high * high), axis=-1, keepdims=True)
    scale = lax.rsqrt(total * (1.0 / C) + 1e-06)

    def silu(values, gain):
        half = 0.5 * (values * scale * gain)
        return half + half * jnp.tanh(half)

    return silu(low, gain_low), silu(high, gain_high)


def twice(high):
    return jnp.concatenate([high, high], axis=-1)


def first_half(lines):
    return lax.broadcasted_iota(jnp.int32, (lines, LO), 1) < 64


def swap(value):
    return pltpu.roll(value, 64, 1)


def join(first, second):
    return jnp.where(first_half(first.shape[0]), first, second)


def split(value):
    mask, other = first_half(value.shape[0]), swap(value)
    return jnp.where(mask, value, other), jnp.where(mask, other, value)


def kernel(sizes, x_hbm, w1_hbm, w2_hbm, g1_hbm, g2_hbm, out,
           x, gains, wlo, whi, wti, elo1, ehi1, elo2, ehi2, taps1, sides1, taps2,
           body_s, body_r, rim_s, rim_r, late_s, late_r,
           load_sem, w_sem, rim_ss, rim_rs, z_ss, z_rs, ready):
    n_tm, n_row, n_col = sizes
    tm, row, col = (lax.axis_index(name) for name in ("tm", "row", "col"))
    scope = jax.named_scope

    def neighbour(dr, dc):
        return (tm, lax.rem(row + (dr + n_row), n_row), lax.rem(col + (dc + n_col), n_col))

    later = (lax.rem(tm + 1, n_tm), row, col)
    earlier = (lax.rem(tm + (n_tm - 1), n_tm), row, col)
    has_later = tm < n_tm - 1
    has_earlier = tm > 0

    barrier = pltpu.get_barrier_semaphore()
    for dr, dc in SIDES:
        pl.semaphore_signal(barrier, inc=1, device_id=neighbour(dr, dc), device_id_type=MESH)

    @pl.when(has_later)
    def _():
        pl.semaphore_signal(barrier, inc=1, device_id=later, device_id_type=MESH)

    loads = [pltpu.make_async_copy(x_hbm, x, load_sem.at[0])]
    for k, g in enumerate((g1_hbm, g2_hbm)):
        loads.append(pltpu.make_async_copy(g, gains.at[k], load_sem.at[k + 1]))
    for load in loads:
        load.start()
    w_loads = []
    for k, w in enumerate((w1_hbm, w2_hbm)):
        group = [
            pltpu.make_async_copy(w.at[:, :, :, 0:128, :], wlo.at[k], w_sem.at[k, 0]),
            pltpu.make_async_copy(w.at[:, :, 0:2, 128:192, :], whi.at[k], w_sem.at[k, 1]),
            pltpu.make_async_copy(w.at[:, :, 2, 128:192, :], wti.at[k, :, 0:3], w_sem.at[k, 2]),
        ]
        for load in group:
            load.start()
        w_loads.append(group)

    wti[:, :, 3] = jnp.zeros((2, 3, 64, C), BF)

    @pl.when(jnp.logical_not(has_earlier))
    def _():
        body_r[...] = jnp.zeros((BODY, LO), BF)
        rim_r[0] = jnp.zeros((RIM, LO), BF)
        late_r[...] = jnp.zeros((LATE, LO), BF)

    keep_row = {-1: jnp.where(row > 0, 1.0, 0.0), 1: jnp.where(row < n_row - 1, 1.0, 0.0)}
    keep_col = {-1: jnp.where(col > 0, 1.0, 0.0), 1: jnp.where(col < n_col - 1, 1.0, 0.0)}

    def side_keep(side):
        dr, dc = SIDES[side]
        if dr and dc:
            return keep_row[dr] * keep_col[dc]
        return keep_row[dr] if dr else keep_col[dc]

    def rim_copy(side):
        here, size = SPOT[side]
        there, _ = SPOT[opposite(side)]
        return pltpu.make_async_remote_copy(
            src_ref=rim_s.at[:, pl.ds(here, size)], dst_ref=rim_r.at[1:3, pl.ds(there, size)],
            send_sem=rim_ss.at[side], recv_sem=rim_rs.at[opposite(side)],
            device_id=neighbour(*SIDES[side]), device_id_type=MESH)

    def z_copy(k):
        src, dst = ((body_s, body_r), (rim_r.at[2], rim_r.at[0]), (late_s, late_r))[k]
        return pltpu.make_async_remote_copy(
            src_ref=src, dst_ref=dst, send_sem=z_ss.at[k], recv_sem=z_rs.at[k],
            device_id=later, device_id_type=MESH)

    def z_start(k):
        pl.when(has_later)(lambda: z_copy(k).start())

    def z_wait(k):
        pl.when(has_earlier)(lambda: z_copy(k).wait_recv())

    def put_body1(frame, low, high):
        for r in range(RO):
            elo1[pl.ds(at1(frame, r + 2, 8), CO)] = low[r * CO:(r + 1) * CO]
            ehi1[pl.ds(at1(frame, r + 2, 8), CO)] = high[r * CO:(r + 1) * CO]

    def pack_rims(pair):
        f = 2 + 2 * pair
        for side, (dr, dc) in enumerate(SIDES):
            spot, _ = SPOT[side]
            r = 2 if dr < 0 else RO
            c = 8 if dc < 0 else 22
            if dc == 0:
                for q in range(2):
                    for i in range(2):
                        to = spot + (2 * i + q) * CO
                        rim_s[pair, to:to + CO] = elo1[pl.ds(at1(f + i, r + q, 8), CO)].astype(BF)
                    high = join(*[ehi1[pl.ds(at1(f + i, r + q, 8), CO)] for i in range(2)])
                    to = spot + 64 + q * CO
                    rim_s[pair, to:to + CO] = high.astype(BF)
            elif dr == 0:
                for i in range(2):
                    low = [elo1[pl.ds(at1(f + i, 2, c + q), RO, stride=EC)] for q in range(2)]
                    to = spot + i * CO
                    rim_s[pair, to:to + CO] = jnp.concatenate(low, axis=0).astype(BF)
                high = [join(*[ehi1[pl.ds(at1(f + i, 2, c + q), RO, stride=EC)] for i in range(2)]) for q in range(2)]
                rim_s[pair, spot + 32:spot + 48] = jnp.concatenate(high, axis=0).astype(BF)
            else:
                pairs = lax.broadcasted_iota(jnp.int32, (8, LO), 0) // 2
                low = high = jnp.zeros((8, LO), F32)
                for i in range(2):
                    for q in range(2):
                        k = 2 * i + q
                        low = jnp.where(pairs == k, elo1[pl.ds(at1(f + i, r + q, c) - 2 * k, 8)], low)
                for q in range(2):
                    both = join(*[ehi1[pl.ds(at1(f + i, r + q, c) - 2 * q, 8)] for i in range(2)])
                    high = jnp.where(pairs == q, both, high)
                rim_s[pair, spot:spot + 16] = jnp.concatenate([low, high], axis=0).astype(BF)

    def put_rims(slot):
        f = 2 * slot
        for side, (dr, dc) in enumerate(SIDES):
            spot, size = SPOT[side]
            r = 0 if dr < 0 else RO + 2
            c = 6 if dc < 0 else 24
            value = rim_r[slot, spot:spot + size].astype(F32) * side_keep(side)
            if dc == 0:
                high = split(value[64:96])
                for i in range(2):
                    for q in range(2):
                        elo1[pl.ds(at1(f + i, r + q, 8), CO)] = value[(2 * i + q) * CO:(2 * i + q + 1) * CO]
                        ehi1[pl.ds(at1(f + i, r + q, 8), CO)] = high[i][q * CO:(q + 1) * CO]
            elif dr == 0:
                high = split(value[32:48])
                for i in range(2):
                    for q in range(2):
                        k = 2 * i + q
                        elo1[pl.ds(at1(f + i, 2, c + q), RO, stride=EC)] = value[k * RO:(k + 1) * RO]
                        ehi1[pl.ds(at1(f + i, 2, c + q), RO, stride=EC)] = high[i][q * RO:(q + 1) * RO]
            else:
                high = split(value[8:16])
                for i in range(2):
                    for q in range(2):
                        k = 2 * i + q
                        elo1[pl.ds(at1(f + i, r + q, c), 2)] = value[2 * k:2 * k + 2]
                        ehi1[pl.ds(at1(f + i, r + q, c), 2)] = high[i][2 * q:2 * q + 2]

    def lanes(low, high, below):
        wide = jnp.concatenate(low + [join(high[0], high[1])], axis=1).astype(BF)
        return wide, join(high[2], below).astype(BF)

    def build1(frame):
        for r in range(ER1):
            low = [elo1[pl.ds(at1(frame, r, 7 + c), CO)] for c in range(3)]
            high = [ehi1[pl.ds(at1(frame, r, 7 + c), CO)] for c in range(3)]
            below = ehi1[pl.ds(at1(frame, min(r + 1, ER1 - 1), 9), CO)]
            wide, tight = lanes(low, high, below)
            taps1[frame, r * CO:(r + 1) * CO, 0:512] = wide
            taps1[frame, r * CO:(r + 1) * CO, 512:640] = tight
        for s, c0 in enumerate((6, 23)):
            lines = slice(s * CO, (s + 1) * CO)
            for b in range(3):
                low = [elo1[pl.ds(at1(frame, b, c0 + c), CO, stride=EC)] for c in range(3)]
                high = [ehi1[pl.ds(at1(frame, b, c0 + c), CO, stride=EC)] for c in range(3)]
                below = high[2]
                if b == 0:
                    below = ehi1[pl.ds(at1(frame, 1, c0 + 2), CO, stride=EC)]
                wide, tight = lanes(low, high, below)
                sides1[frame, lines, b * 512:(b + 1) * 512] = wide
                if b != 1:
                    sides1[frame, lines, 1536 + b * 64:1664 + b * 64] = tight

    def build2(frame):
        for r in range(ER2):
            low = [elo2[pl.ds(at2(frame, r, 7 + c), CO)] for c in range(3)]
            high = [ehi2[pl.ds(at2(frame, r, 7 + c), CO)] for c in range(3)]
            below = ehi2[pl.ds(at2(frame, min(r + 1, ER2 - 1), 9), CO)]
            wide, tight = lanes(low, high, below)
            taps2[frame, r * CO:(r + 1) * CO, 0:512] = wide
            taps2[frame, r * CO:(r + 1) * CO, 512:640] = tight

    def conv(k, a, frame):
        f = frame - 2 + a
        taps, rows = ((taps1, ER2), (taps2, RO))[k]
        count = rows * CO
        left = [taps[f:f + 2, b * CO:b * CO + count, 0:512].reshape(2 * count, 512) for b in range(3)]
        left += [taps[f:f + 2, b * CO:b * CO + count, 512:640].reshape(2 * count, LO) for b in (0, 2)]
        left = jnp.concatenate(left, axis=1)
        if k == 0:
            left = jnp.concatenate([left, sides1[f:f + 2].reshape(2 * SIDE, 14 * LO)], axis=0)
        right = []
        for b in range(3):
            right += [wlo[k, a, b].reshape(3 * LO, C), whi[k, a, b].reshape(LO, C)]
        right.append(wti[k, a].reshape(2 * LO, C))
        return jnp.dot(left, jnp.concatenate(right, axis=0), preferred_element_type=F32)

    def put2(frame, low, high):
        for i in range(2):
            for r in range(ER2):
                lines = slice(i * MAIN + r * CO, i * MAIN + (r + 1) * CO)
                elo2[pl.ds(at2(frame + i, r, 8), CO)] = low[lines]
                ehi2[pl.ds(at2(frame + i, r, 8), CO)] = high[lines]
            for s, c in enumerate((7, 24)):
                here = 2 * MAIN + i * SIDE + s * CO
                for first, count in ((0, 8), (8, 2)):
                    lines = slice(here + first, here + first + count)
                    elo2[pl.ds(at2(frame + i, first, c), count, stride=EC)] = low[lines]
                    ehi2[pl.ds(at2(frame + i, first, c), count, stride=EC)] = high[lines]

    def inside(value):
        parts = []
        for i in range(2):
            here = i * MAIN
            parts.append(value[here:here + CO] * keep_row[-1])
            parts.append(value[here + CO:here + MAIN - CO])
            parts.append(value[here + MAIN - CO:here + MAIN] * keep_row[1])
        lines = lax.broadcasted_iota(jnp.int32, (CO, LO), 0)
        factor = jnp.where(lines == 0, keep_row[-1], jnp.where(lines == ER2 - 1, keep_row[1], 1.0))
        for i in range(2):
            for s, dc in enumerate((-1, 1)):
                here = 2 * MAIN + i * SIDE + s * CO
                parts.append(value[here:here + CO] * (factor * keep_col[dc]))
        return jnp.concatenate(parts, axis=0)

    def finish_first(total):
        low, high = norm_act(total[:, :LO], twice(total[:, LO:]), *gain[1])
        return inside(low), inside(high)

    def finish_second(frame, total):
        f = frame - 2
        total = total + x[f:f + 2].reshape(2 * PX, C).astype(F32)
        out[f:f + 2] = total.astype(BF).reshape(2, RO, CO, C)

    with scope("load"):
        for load in loads:
            load.wait()
        gain = []
        for k in range(2):
            value = gains[k]
            gain.append((value[:, :LO], twice(value[:, LO:])))
    with scope("norm"):
        kept = {}
        for f in (2, 3, 0, 1):
            value = x[f].reshape(PX, C).astype(F32)
            low, high = norm_act(value[:, :LO], twice(value[:, LO:]), *gain[0])
            put_body1(f + 2, low, high)
            kept[f] = low, high
        pack_rims(1)
        pack_rims(0)
        for i in range(2):
            body_s[i * PX:(i + 1) * PX] = kept[2 + i][0].astype(BF)
        body_s[2 * PX:3 * PX] = join(kept[2][1], kept[3][1]).astype(BF)

    with scope("barrier"):
        pl.semaphore_wait(barrier, jnp.where(has_earlier, 9, 8))

        @pl.when(has_earlier)
        def _():
            pl.semaphore_signal(ready, inc=1, device_id=earlier, device_id_type=MESH)
    with scope("send_rims"):
        for side in range(8):
            rim_copy(side).start()
    with scope("send_cache"):
        @pl.when(has_later)
        def _():
            pl.semaphore_wait(ready, 1)
            z_copy(0).start()

    with scope("wait_rims"):
        for side in range(8):
            rim_copy(opposite(side)).wait_recv()
        z_start(1)
    with scope("build_own"):
        put_rims(2)
        build1(4)
        build1(5)
        put_rims(1)
        build1(2)
        build1(3)
    with scope("wait_weights"):
        for load in w_loads[0]:
            load.wait()
    with scope("conv_first"):
        low, high = finish_first(conv(0, 0, 4) + conv(0, 1, 4) + conv(0, 2, 4))
        count = 2 * (MAIN + SIDE)
        late_s[0:count] = low.astype(BF)
        late_s[count:count + MAIN] = join(high[0:MAIN], high[MAIN:2 * MAIN]).astype(BF)
        late_s[count + MAIN:LATE] = join(high[2 * MAIN:2 * MAIN + SIDE], high[2 * MAIN + SIDE:]).astype(BF)
        z_start(2)
        put2(4, low, high)
        total = conv(0, 2, 2)

    with scope("wait_cache"):
        z_wait(0)
        z_wait(1)
    with scope("build_cache"):
        low, high = body_r[0:2 * PX].astype(F32), split(body_r[2 * PX:3 * PX].astype(F32))
        for i in range(2):
            put_body1(i, low[i * PX:(i + 1) * PX], high[i])
        put_rims(0)
        build1(0)
        build1(1)
    with scope("conv_first_early"):
        low, high = finish_first(total + conv(0, 1, 2) + conv(0, 0, 2))
        put2(2, low, high)

    with scope("build_second"):
        for f in (2, 3, 4, 5):
            build2(f)
    with scope("wait_weights"):
        for load in w_loads[1]:
            load.wait()
    with scope("conv_second"):
        finish_second(4, conv(1, 0, 4) + conv(1, 1, 4) + conv(1, 2, 4))
        total = conv(1, 2, 2)

    with scope("wait_late"):
        z_wait(2)
    with scope("build_late"):
        count = 2 * (MAIN + SIDE)
        low = late_r[0:count].astype(F32)
        main = split(late_r[count:count + MAIN].astype(F32))
        beside = split(late_r[count + MAIN:LATE].astype(F32))
        put2(0, low, jnp.concatenate([*main, *beside], axis=0))
        build2(0)
        build2(1)
    with scope("conv_late"):
        finish_second(2, total + conv(1, 1, 2) + conv(1, 0, 2))

    with scope("drain"):
        for side in range(8):
            rim_copy(side).wait_send()

        @pl.when(has_later)
        def _():
            for k in range(3):
                z_copy(k).wait_send()


def solution(mesh):
    sizes = tuple(mesh.shape[name] for name in ("tm", "row", "col"))

    def shards(features, conv_first, conv_second, gain_first, gain_second):
        in_hbm = pl.BlockSpec(memory_space=pltpu.HBM)
        dma = pltpu.SemaphoreType.DMA
        return pl.pallas_call(
            functools.partial(kernel, sizes),
            out_shape=pltpu.VMEM(features.shape, BF),
            in_specs=[in_hbm] * 5,
            out_specs=pl.BlockSpec(memory_space=pltpu.VMEM),
            scratch_shapes=[
                pltpu.VMEM((FR, RO, CO, C), BF),
                pltpu.VMEM((2, 1, C), F32),
                pltpu.VMEM((2, 3, 3, 3, LO, C), BF),
                pltpu.VMEM((2, 3, 3, 2, 64, C), BF),
                pltpu.VMEM((2, 3, 4, 64, C), BF),
                pltpu.VMEM(((EF + 1) * ER1 * EC, LO), F32),
                pltpu.VMEM(((EF + 1) * ER1 * EC, LO), F32),
                pltpu.VMEM((EF * ER2 * EC, LO), F32),
                pltpu.VMEM((EF * ER2 * EC, LO), F32),
                pltpu.VMEM((EF, ER1 * CO, 5 * LO), BF),
                pltpu.VMEM((EF, SIDE, 14 * LO), BF),
                pltpu.VMEM((EF, ER2 * CO, 5 * LO), BF),
                pltpu.VMEM((BODY, LO), BF),
                pltpu.VMEM((BODY, LO), BF),
                pltpu.VMEM((2, RIM, LO), BF),
                pltpu.VMEM((3, RIM, LO), BF),
                pltpu.VMEM((LATE, LO), BF),
                pltpu.VMEM((LATE, LO), BF),
                dma((3,)), dma((2, 3)), dma((8,)), dma((8,)), dma((3,)), dma((3,)), pltpu.SemaphoreType.REGULAR,
            ],
            compiler_params=pltpu.CompilerParams(
                collective_id=0, has_side_effects=True, vmem_limit_bytes=60 * 1024 * 1024),
        )(features, conv_first, conv_second, gain_first.reshape(1, C), gain_second.reshape(1, C))

    return jax.shard_map(
        shards, mesh=mesh, in_specs=(P("tm", "row", "col", None), P(), P(), P(), P()),
        out_specs=P("tm", "row", "col", None), check_vma=False)
```

time: 93.4 us -> 23.6 us (0.25)
  the two profiles are of different devices: /device:TPU:259 before, /device:TPU:1 now
where the time goes in v2:
time: 23.6 us; the launch traced here: 23.5 us
  Pallas kernels  22.8 us (97%)
  local copies, waits for them, and re-layouts  0.71 us (3%)
    pallas_call x1, Pallas kernels, shards(): pl.pallas_call(functools.partial(kernel, sizes), out_shape=pltpu.VMEM(fea...  22.8 us
    unnamed x1, local copies, waits for them, and re-layouts  0.71 us

profile of v2, /device:TPU:1, one launch (start us, length us, event | category | flops | bytes accessed | tf_op | source)
XLA Modules:
  0.0 23.5 jit_solution(10798406361553816011)
XLA Ops:
  0.0 22.8 %shard_map.55 = bf16[4,8,16,192]{3,2,1,0:T(8,128)(2,1)S(1)} custom-call(bf16[4,8,16,192]{3,2,1,0:T(8,128)(2,1)} %x_hbm.1, bf16[3,3,3,192,192]{4,3,2,1,0:T(8,128)(2,1)} %w1_hbm.1, bf16[3,3,3,192,192]{4,3,2,1,0:T(8,128)(2,1)} %w2_hbm.1, f32[1,192]{1,0:T(1,128)} %bitcast.2, f32[1,192]{1,0:T(1,128)} %bitcast.3), custom_call_target="tpu_custom_call" | custom-call | tf_op jit(solution)/shard_map/pallas_call | solution.py:412
  22.8 0.7 %copy.7 = bf16[4,8,16,192]{3,2,1,0:T(8,128)(2,1)} copy(bf16[4,8,16,192]{3,2,1,0:T(8,128)(2,1)S(1)} %shard_map.55) | data formatting | bytes 393216

commit v3 on v2

v3 whole, which is shorter than its diff:
```python
import functools

import jax
import jax.numpy as jnp
from jax import lax
from jax.experimental import pallas as pl
from jax.experimental.pallas import tpu as pltpu
from jax.sharding import PartitionSpec as P

MESH = pl.DeviceIdType.MESH
BF = jnp.bfloat16
F32 = jnp.float32
C = 192
LO = 128
FR, RO, CO = 4, 8, 16
PX = RO * CO
EF, ER1, ER2, EC = 6, 12, 10, 32
MAIN, SIDE = ER2 * CO, 2 * CO
EDGE = (6, 7, 8, 23, 24, 25)
EL = 32
SIDES = ((-1, 0), (1, 0), (0, -1), (0, 1), (-1, -1), (-1, 1), (1, -1), (1, 1))
SPOT = ((0, 96), (96, 96), (192, 48), (240, 48), (288, 16), (304, 16), (320, 16), (336, 16))
RIM = 352
BODY = 3 * PX
LINES = MAIN + SIDE
LATE = LINES * 3 // 2


def opposite(side):
    dr, dc = SIDES[side]
    return SIDES.index((-dr, -dc))


def at1(frame, row, col):
    return (frame * ER1 + row) * EC + col


def edge(frame, row, col):
    return (frame * len(EDGE) + EDGE.index(col)) * EL + row + 6


def at2(frame, row, col):
    return (frame * ER2 + row) * EC + col


def norm_act(low, high, gain_low, gain_high):
    total = jnp.sum(low * low + 0.5 * (high * high), axis=-1, keepdims=True)
    scale = lax.rsqrt(total * (1.0 / C) + 1e-06)

    def silu(values, gain):
        half = values * scale * gain
        return half + half * jnp.tanh(half)

    return silu(low, gain_low), silu(high, gain_high)


def twice(high):
    return jnp.concatenate([high, high], axis=-1)


def first_half(lines):
    return lax.broadcasted_iota(jnp.int32, (lines, LO), 1) < 64


def swap(value):
    return pltpu.roll(value, 64, 1)


def join(first, second):
    return jnp.where(first_half(first.shape[0]), first, second)


def split(value):
    mask, other = first_half(value.shape[0]), swap(value)
    return jnp.where(mask, value, other), jnp.where(mask, other, value)


def kernel(sizes, x_hbm, w1_hbm, w2_hbm, g1_hbm, g2_hbm, out,
           x, gains, wlo, whi, wti, elo1, ehi1, vlo, vhi, elo2, ehi2, taps1, sides1, taps2, sums1, sums2,
           body_s, body_r, rim_s, rim_r, late_s, late_r,
           load_sem, w_sem, rim_ss, rim_rs, z_ss, z_rs):
    n_tm, n_row, n_col = sizes
    tm, row, col = (lax.axis_index(name) for name in ("tm", "row", "col"))
    scope = jax.named_scope

    def neighbour(dr, dc):
        return (tm, lax.rem(row + (dr + n_row), n_row), lax.rem(col + (dc + n_col), n_col))

    later = (lax.rem(tm + 1, n_tm), row, col)
    earlier = (lax.rem(tm + (n_tm - 1), n_tm), row, col)
    has_later = tm < n_tm - 1
    has_earlier = tm > 0

    barrier = pltpu.get_barrier_semaphore()
    for dr, dc in SIDES:
        pl.semaphore_signal(barrier, inc=1, device_id=neighbour(dr, dc), device_id_type=MESH)

    @pl.when(has_earlier)
    def _():
        pl.semaphore_signal(barrier, inc=1, device_id=earlier, device_id_type=MESH)

    loads = [pltpu.make_async_copy(x_hbm, x, load_sem.at[0])]
    for k, g in enumerate((g1_hbm, g2_hbm)):
        loads.append(pltpu.make_async_copy(g, gains.at[k], load_sem.at[k + 1]))
    for load in loads:
        load.start()
    w_loads = []
    for k, w in enumerate((w1_hbm, w2_hbm)):
        group = [
            pltpu.make_async_copy(w.at[:, :, :, 0:128, :], wlo.at[k], w_sem.at[k, 0]),
            pltpu.make_async_copy(w.at[:, :, 0:2, 128:192, :], whi.at[k], w_sem.at[k, 1]),
            pltpu.make_async_copy(w.at[:, :, 2, 128:192, :], wti.at[k, :, 0:3], w_sem.at[k, 2]),
        ]
        for load in group:
            load.start()
        w_loads.append(group)

    wti[:, :, 3] = jnp.zeros((2, 3, 64, C), BF)

    @pl.when(jnp.logical_not(has_earlier))
    def _():
        body_r[...] = jnp.zeros((BODY, LO), BF)
        rim_r[0] = jnp.zeros((RIM, LO), BF)
        late_r[...] = jnp.zeros((2, LATE, LO), BF)

    keep_row = {-1: jnp.where(row > 0, 1.0, 0.0), 1: jnp.where(row < n_row - 1, 1.0, 0.0)}
    keep_col = {-1: jnp.where(col > 0, 1.0, 0.0), 1: jnp.where(col < n_col - 1, 1.0, 0.0)}

    def side_keep(side):
        dr, dc = SIDES[side]
        if dr and dc:
            return keep_row[dr] * keep_col[dc]
        return keep_row[dr] if dr else keep_col[dc]

    def rim_copy(side):
        here, size = SPOT[side]
        there, _ = SPOT[opposite(side)]
        return pltpu.make_async_remote_copy(
            src_ref=rim_s.at[:, pl.ds(here, size)], dst_ref=rim_r.at[1:3, pl.ds(there, size)],
            send_sem=rim_ss.at[side], recv_sem=rim_rs.at[opposite(side)],
            device_id=neighbour(*SIDES[side]), device_id_type=MESH)

    def z_copy(k):
        src, dst = (
            (body_s, body_r), (rim_r.at[2], rim_r.at[0]),
            (late_s.at[0], late_r.at[0]), (late_s.at[1], late_r.at[1]))[k]
        return pltpu.make_async_remote_copy(
            src_ref=src, dst_ref=dst, send_sem=z_ss.at[k], recv_sem=z_rs.at[k],
            device_id=later, device_id_type=MESH)

    def z_start(k):
        pl.when(has_later)(lambda: z_copy(k).start())

    def z_wait(k):
        pl.when(has_earlier)(lambda: z_copy(k).wait_recv())

    def put_body1(frame, low, high):
        for r in range(RO):
            elo1[pl.ds(at1(frame, r + 2, 8), CO)] = low[r * CO:(r + 1) * CO]
            ehi1[pl.ds(at1(frame, r + 2, 8), CO)] = high[r * CO:(r + 1) * CO]

    def pack_rims(pair):
        f = 2 + 2 * pair
        for side, (dr, dc) in enumerate(SIDES):
            spot, _ = SPOT[side]
            r = 2 if dr < 0 else RO
            c = 8 if dc < 0 else 22
            if dc == 0:
                for q in range(2):
                    for i in range(2):
                        to = spot + (2 * i + q) * CO
                        rim_s[pair, to:to + CO] = elo1[pl.ds(at1(f + i, r + q, 8), CO)].astype(BF)
                    high = join(*[ehi1[pl.ds(at1(f + i, r + q, 8), CO)] for i in range(2)])
                    to = spot + 64 + q * CO
                    rim_s[pair, to:to + CO] = high.astype(BF)
            elif dr == 0:
                outer = 0 if dc < 0 else 1
                high = []
                for i in range(2):
                    low = [elo1[pl.ds(at1(f + i, 2, c + q), RO, stride=EC)] for q in range(2)]
                    high.append([ehi1[pl.ds(at1(f + i, 2, c + q), RO, stride=EC)] for q in range(2)])
                    to = spot + i * CO
                    rim_s[pair, to:to + CO] = jnp.concatenate(low, axis=0).astype(BF)
                    vlo[pl.ds(edge(f + i, 2, c + outer), RO)] = low[outer]
                    vhi[pl.ds(edge(f + i, 2, c + outer), RO)] = high[i][outer]
                both = [join(high[0][q], high[1][q]) for q in range(2)]
                rim_s[pair, spot + 32:spot + 48] = jnp.concatenate(both, axis=0).astype(BF)
            else:
                pairs = lax.broadcasted_iota(jnp.int32, (8, LO), 0) // 2
                low = high = jnp.zeros((8, LO), F32)
                for i in range(2):
                    for q in range(2):
                        k = 2 * i + q
                        low = jnp.where(pairs == k, elo1[pl.ds(at1(f + i, r + q, c) - 2 * k, 8)], low)
                for q in range(2):
                    both = join(*[ehi1[pl.ds(at1(f + i, r + q, c) - 2 * q, 8)] for i in range(2)])
                    high = jnp.where(pairs == q, both, high)
                rim_s[pair, spot:spot + 16] = jnp.concatenate([low, high], axis=0).astype(BF)

    def put_rims(slot):
        f = 2 * slot
        for side, (dr, dc) in enumerate(SIDES):
            spot, size = SPOT[side]
            r = 0 if dr < 0 else RO + 2
            c = 6 if dc < 0 else 24
            value = rim_r[slot, spot:spot + size].astype(F32) * side_keep(side)
            near = 1 if dc < 0 else 0
            for i in range(2):
                for q in range(2):
                    k = 2 * i + q
                    if dc == 0:
                        low, high = value[k * CO:(k + 1) * CO], split(value[64:96])[i][q * CO:(q + 1) * CO]
                        elo1[pl.ds(at1(f + i, r + q, 8), CO)] = low
                        ehi1[pl.ds(at1(f + i, r + q, 8), CO)] = high
                        for line, border in ((0, 8), (CO - 1, 23)):
                            vlo[pl.ds(edge(f + i, r + q, border), 1)] = low[line:line + 1]
                            vhi[pl.ds(edge(f + i, r + q, border), 1)] = high[line:line + 1]
                    elif dr == 0:
                        low, high = value[k * RO:(k + 1) * RO], split(value[32:48])[i][q * RO:(q + 1) * RO]
                        vlo[pl.ds(edge(f + i, 2, c + q), RO)] = low
                        vhi[pl.ds(edge(f + i, 2, c + q), RO)] = high
                        if q == near:
                            elo1[pl.ds(at1(f + i, 2, c + q), RO, stride=EC)] = low
                            ehi1[pl.ds(at1(f + i, 2, c + q), RO, stride=EC)] = high
                    else:
                        low, high = value[2 * k:2 * k + 2], split(value[8:16])[i][2 * q:2 * q + 2]
                        for j in range(2):
                            vlo[pl.ds(edge(f + i, r + q, c + j), 1)] = low[j:j + 1]
                            vhi[pl.ds(edge(f + i, r + q, c + j), 1)] = high[j:j + 1]
                        elo1[pl.ds(at1(f + i, r + q, c + near), 1)] = low[near:near + 1]
                        ehi1[pl.ds(at1(f + i, r + q, c + near), 1)] = high[near:near + 1]

    def lanes(low, high, below):
        wide = jnp.concatenate(low + [join(high[0], high[1])], axis=1).astype(BF)
        return wide, join(high[2], below).astype(BF)

    def build(elo, ehi, at, rows, taps, frame):
        last = ehi[pl.ds(at(frame, rows - 1, 9), CO)]
        for r in reversed(range(rows)):
            low = [elo[pl.ds(at(frame, r, 7 + c), CO)] for c in range(3)]
            high = [ehi[pl.ds(at(frame, r, 7 + c), CO)] for c in range(2)]
            high.append(last if r == rows - 1 else ehi[pl.ds(at(frame, r, 9), CO)])
            wide, tight = lanes(low, high, last)
            last = high[2]
            taps[frame, r * CO:(r + 1) * CO, 0:512] = wide
            taps[frame, r * CO:(r + 1) * CO, 512:640] = tight

    def build1(frame):
        build(elo1, ehi1, at1, ER1, taps1, frame)
        for s in range(2):
            lines = slice(s * CO, (s + 1) * CO)
            cols = EDGE[3 * s:3 * s + 3]
            low = [[vlo[pl.ds(edge(frame, b, c), CO)] for c in cols] for b in range(3)]
            high = [[vhi[pl.ds(edge(frame, b, c), CO)] for c in cols] for b in range(3)]
            for b in range(3):
                wide, tight = lanes(low[b], high[b], high[min(b + 1, 2)][2])
                sides1[frame, lines, b * 512:(b + 1) * 512] = wide
                if b != 1:
                    sides1[frame, lines, 1536 + b * 64:1664 + b * 64] = tight

    def build2(frame):
        build(elo2, ehi2, at2, ER2, taps2, frame)

    def conv(k, jobs, halves=False):
        taps, count, sums = ((taps1, MAIN, sums1), (taps2, PX, sums2))[k]
        for target, a in jobs:
            f = target - 2 + a
            left = [taps[f, b * CO:b * CO + count, 0:512] for b in range(3)]
            left += [taps[f, b * CO:b * CO + count, 512:640] for b in (0, 2)]
            left = jnp.concatenate(left, axis=1)
            if k == 0:
                left = jnp.concatenate([left, sides1[f]], axis=0)
            right = []
            for b in range(3):
                right += [wlo[k, a, b].reshape(3 * LO, C), whi[k, a, b].reshape(LO, C)]
            right = jnp.concatenate(right + [wti[k, a].reshape(2 * LO, C)], axis=0)
            size = left.shape[0] // 2 if halves else left.shape[0]
            for here in range(0, left.shape[0], size):
                part = jnp.dot(left[here:here + size], right, preferred_element_type=F32)
                if (k, target) in begun:
                    part = part + sums[target - 2, here:here + size]
                sums[target - 2, here:here + size] = part
            begun.add((k, target))

    begun = set()

    def put2(frame, low, high):
        for r in range(ER2):
            lines = slice(r * CO, (r + 1) * CO)
            elo2[pl.ds(at2(frame, r, 8), CO)] = low[lines]
            ehi2[pl.ds(at2(frame, r, 8), CO)] = high[lines]
        for s, c in enumerate((7, 24)):
            for first, count in ((0, 8), (8, 2)):
                lines = slice(MAIN + s * CO + first, MAIN + s * CO + first + count)
                elo2[pl.ds(at2(frame, first, c), count, stride=EC)] = low[lines]
                ehi2[pl.ds(at2(frame, first, c), count, stride=EC)] = high[lines]

    def inside(value):
        parts = [value[0:CO] * keep_row[-1], value[CO:MAIN - CO], value[MAIN - CO:MAIN] * keep_row[1]]
        lines = lax.broadcasted_iota(jnp.int32, (CO, LO), 0)
        factor = jnp.where(lines == 0, keep_row[-1], jnp.where(lines == ER2 - 1, keep_row[1], 1.0))
        for s, dc in enumerate((-1, 1)):
            parts.append(value[MAIN + s * CO:MAIN + (s + 1) * CO] * (factor * keep_col[dc]))
        return jnp.concatenate(parts, axis=0)

    def finish_first(frame):
        total = sums1[frame - 2]
        low, high = norm_act(total[:, :LO], twice(total[:, LO:]), *gain[1])
        return inside(low), inside(high)

    def finish_second(frame):
        f = frame - 2
        total = sums2[f] + x[f].reshape(PX, C).astype(F32)
        out[f] = total.astype(BF).reshape(RO, CO, C)

    def pack_late(i, low, high):
        late_s[i, 0:LINES] = low.astype(BF)
        late_s[i, LINES:LINES + 80] = join(high[0:80], high[80:160]).astype(BF)
        late_s[i, LINES + 80:LATE] = join(high[160:176], high[176:192]).astype(BF)

    def put_late(i):
        low = late_r[i, 0:LINES].astype(F32)
        main = split(late_r[i, LINES:LINES + 80].astype(F32))
        beside = split(late_r[i, LINES + 80:LATE].astype(F32))
        put2(i, low, jnp.concatenate([*main, *beside], axis=0))

    with scope("load"):
        for load in loads:
            load.wait()
        gain = []
        for k in range(2):
            value = 0.5 * gains[k]
            gain.append((value[:, :LO], twice(value[:, LO:])))
    with scope("norm"):
        kept = {}
        for f in (2, 3, 0, 1):
            value = x[f].reshape(PX, C).astype(F32)
            low, high = norm_act(value[:, :LO], twice(value[:, LO:]), *gain[0])
            put_body1(f + 2, low, high)
            kept[f] = low, high
        pack_rims(1)
        pack_rims(0)
        for i in range(2):
            body_s[i * PX:(i + 1) * PX] = kept[2 + i][0].astype(BF)
        body_s[2 * PX:3 * PX] = join(kept[2][1], kept[3][1]).astype(BF)

    with scope("barrier"):
        pl.semaphore_wait(barrier, jnp.where(has_later, 9, 8))
    with scope("send_rims"):
        for side in reversed(range(8)):
            rim_copy(side).start()
    with scope("send_cache"):
        z_start(0)

    with scope("wait_rims"):
        for side in range(8):
            rim_copy(opposite(side)).wait_recv()
        z_start(1)
    with scope("build_own"):
        put_rims(2)
        build1(4)
        build1(5)
        put_rims(1)
        build1(2)
        build1(3)
    with scope("wait_weights"):
        for load in w_loads[0]:
            load.wait()
    with scope("conv_first"):
        conv(0, ((5, 0), (4, 0), (5, 1), (4, 1), (5, 2), (4, 2)))
        kept = {}
        for f in (5, 4):
            kept[f] = finish_first(f)
            pack_late(f - 4, *kept[f])
    with scope("send_late"):
        z_start(3)
        z_start(2)
    with scope("conv_ahead"):
        conv(0, ((2, 2), (3, 2)))
        conv(0, ((3, 1),), halves=True)
        for f in (4, 5):
            put2(f, *kept[f])
            build2(f)
        for load in w_loads[1]:
            load.wait()
        conv(1, ((4, 2), (5, 2)))
        conv(1, ((5, 1),), halves=True)

    with scope("wait_cache"):
        z_wait(0)
        z_wait(1)
    with scope("build_cache"):
        low, high = body_r[0:2 * PX].astype(F32), split(body_r[2 * PX:3 * PX].astype(F32))
        for i in range(2):
            put_body1(i, low[i * PX:(i + 1) * PX], high[i])
            for border in (8, 23):
                vlo[pl.ds(edge(i, 2, border), RO)] = elo1[pl.ds(at1(i, 2, border), RO, stride=EC)]
                vhi[pl.ds(edge(i, 2, border), RO)] = ehi1[pl.ds(at1(i, 2, border), RO, stride=EC)]
        put_rims(0)
        build1(0)
        build1(1)
    with scope("conv_first_early"):
        conv(0, ((2, 0), (3, 0)))
        conv(0, ((2, 1),), halves=True)
        for f in (2, 3):
            put2(f, *finish_first(f))
            build2(f)
    with scope("conv_second"):
        conv(1, ((4, 0), (5, 0), (4, 1), (3, 1), (2, 2), (3, 2)))
        finish_second(4)
        finish_second(5)

    with scope("wait_late"):
        z_wait(3)
    with scope("conv_late"):
        put_late(1)
        build2(1)
        conv(1, ((3, 0), (2, 1)))
        finish_second(3)
    with scope("wait_last"):
        z_wait(2)
    with scope("conv_last"):
        put_late(0)
        build2(0)
        conv(1, ((2, 0),), halves=True)
        finish_second(2)

    with scope("drain"):
        for side in range(8):
            rim_copy(side).wait_send()

        @pl.when(has_later)
        def _():
            for k in range(4):
                z_copy(k).wait_send()


def solution(mesh):
    sizes = tuple(mesh.shape[name] for name in ("tm", "row", "col"))

    def shards(features, conv_first, conv_second, gain_first, gain_second):
        in_hbm = pl.BlockSpec(memory_space=pltpu.HBM)
        dma = pltpu.SemaphoreType.DMA
        return pl.pallas_call(
            functools.partial(kernel, sizes),
            out_shape=pltpu.VMEM(features.shape, BF),
            in_specs=[in_hbm] * 5,
            out_specs=pl.BlockSpec(memory_space=pltpu.VMEM),
            scratch_shapes=[
                pltpu.VMEM((FR, RO, CO, C), BF),
                pltpu.VMEM((2, 1, C), F32),
                pltpu.VMEM((2, 3, 3, 3, LO, C), BF),
                pltpu.VMEM((2, 3, 3, 2, 64, C), BF),
                pltpu.VMEM((2, 3, 4, 64, C), BF),
                pltpu.VMEM((EF * ER1 * EC, LO), F32),
                pltpu.VMEM((EF * ER1 * EC, LO), F32),
                pltpu.VMEM((EF * len(EDGE) * EL, LO), F32),
                pltpu.VMEM((EF * len(EDGE) * EL, LO), F32),
                pltpu.VMEM((EF * ER2 * EC, LO), F32),
                pltpu.VMEM((EF * ER2 * EC, LO), F32),
                pltpu.VMEM((EF, ER1 * CO, 5 * LO), BF),
                pltpu.VMEM((EF, SIDE, 14 * LO), BF),
                pltpu.VMEM((EF, ER2 * CO, 5 * LO), BF),
                pltpu.VMEM((FR, MAIN + SIDE, C), F32),
                pltpu.VMEM((FR, PX, C), F32),
                pltpu.VMEM((BODY, LO), BF),
                pltpu.VMEM((BODY, LO), BF),
                pltpu.VMEM((2, RIM, LO), BF),
                pltpu.VMEM((3, RIM, LO), BF),
                pltpu.VMEM((2, LATE, LO), BF),
                pltpu.VMEM((2, LATE, LO), BF),
                dma((3,)), dma((2, 3)), dma((8,)), dma((8,)), dma((4,)), dma((4,)),
            ],
            compiler_params=pltpu.CompilerParams(
                collective_id=0, has_side_effects=True, vmem_limit_bytes=60 * 1024 * 1024),
        )(features, conv_first, conv_second, gain_first.reshape(1, C), gain_second.reshape(1, C))

    return jax.shard_map(
        shards, mesh=mesh, in_specs=(P("tm", "row", "col", None), P(), P(), P(), P()),
        out_specs=P("tm", "row", "col", None), check_vma=False)
```

time: 23.6 us -> 20.3 us (0.86)
  the two profiles are of different devices: /device:TPU:1 before, /device:TPU:32 now
where the time goes in v3:
time: 20.3 us; the launch traced here: 20.2 us
  Pallas kernels  19.5 us (96%)
  local copies, waits for them, and re-layouts  0.71 us (3%)
    pallas_call x1, Pallas kernels, shards(): pl.pallas_call(functools.partial(kernel, sizes), out_shape=pltpu.VMEM(fea...  19.5 us
    unnamed x1, local copies, waits for them, and re-layouts  0.71 us

profile of v3, /device:TPU:32, one launch (start us, length us, event | category | flops | bytes accessed | tf_op | source)
XLA Modules:
  0.0 20.2 jit_solution(1645251729544569022)
XLA Ops:
  0.0 19.5 %shard_map.55 = bf16[4,8,16,192]{3,2,1,0:T(8,128)(2,1)S(1)} custom-call(bf16[4,8,16,192]{3,2,1,0:T(8,128)(2,1)} %x_hbm.1, bf16[3,3,3,192,192]{4,3,2,1,0:T(8,128)(2,1)} %w1_hbm.1, bf16[3,3,3,192,192]{4,3,2,1,0:T(8,128)(2,1)} %w2_hbm.1, f32[1,192]{1,0:T(1,128)} %bitcast.2, f32[1,192]{1,0:T(1,128)} %bitcast.3), custom_call_target="tpu_custom_call" | custom-call | tf_op jit(solution)/shard_map/pallas_call | solution.py:444
  19.5 0.7 %copy.7 = bf16[4,8,16,192]{3,2,1,0:T(8,128)(2,1)} copy(bf16[4,8,16,192]{3,2,1,0:T(8,128)(2,1)S(1)} %shard_map.55) | data formatting | bytes 393216

commit v4 on v3

--- a/solution.py
+++ b/solution.py
@@ -22,8 +22,6 @@
 SPOT = ((0, 96), (96, 96), (192, 48), (240, 48), (288, 16), (304, 16), (320, 16), (336, 16))
 RIM = 352
 BODY = 3 * PX
-LINES = MAIN + SIDE
-LATE = LINES * 3 // 2
 
 
 def opposite(side):
@@ -119,9 +117,7 @@
 
     @pl.when(jnp.logical_not(has_earlier))
     def _():
-        body_r[...] = jnp.zeros((BODY, LO), BF)
-        rim_r[0] = jnp.zeros((RIM, LO), BF)
-        late_r[...] = jnp.zeros((2, LATE, LO), BF)
+        late_r[...] = jnp.zeros((BODY, LO), BF)
 
     keep_row = {-1: jnp.where(row > 0, 1.0, 0.0), 1: jnp.where(row < n_row - 1, 1.0, 0.0)}
     keep_col = {-1: jnp.where(col > 0, 1.0, 0.0), 1: jnp.where(col < n_col - 1, 1.0, 0.0)}
@@ -141,9 +137,7 @@
             device_id=neighbour(*SIDES[side]), device_id_type=MESH)
 
     def z_copy(k):
-        src, dst = (
-            (body_s, body_r), (rim_r.at[2], rim_r.at[0]),
-            (late_s.at[0], late_r.at[0]), (late_s.at[1], late_r.at[1]))[k]
+        src, dst = ((body_s, body_r), (rim_r.at[2], rim_r.at[0]), (late_s, late_r))[k]
         return pltpu.make_async_remote_copy(
             src_ref=src, dst_ref=dst, send_sem=z_ss.at[k], recv_sem=z_rs.at[k],
             device_id=later, device_id_type=MESH)
@@ -261,26 +255,41 @@
     def build2(frame):
         build(elo2, ehi2, at2, ER2, taps2, frame)
 
-    def conv(k, jobs, halves=False):
-        taps, count, sums = ((taps1, MAIN, sums1), (taps2, PX, sums2))[k]
-        for target, a in jobs:
-            f = target - 2 + a
-            left = [taps[f, b * CO:b * CO + count, 0:512] for b in range(3)]
-            left += [taps[f, b * CO:b * CO + count, 512:640] for b in (0, 2)]
-            left = jnp.concatenate(left, axis=1)
+    def products(k, a, frames, pieces=1):
+        taps, count = ((taps1, MAIN), (taps2, PX))[k]
+        left = []
+        for f in frames:
+            parts = [taps[f, b * CO:b * CO + count, 0:512] for b in range(3)]
+            parts += [taps[f, b * CO:b * CO + count, 512:640] for b in (0, 2)]
+            left.append(jnp.concatenate(parts, axis=1))
             if k == 0:
-                left = jnp.concatenate([left, sides1[f]], axis=0)
-            right = []
-            for b in range(3):
-                right += [wlo[k, a, b].reshape(3 * LO, C), whi[k, a, b].reshape(LO, C)]
-            right = jnp.concatenate(right + [wti[k, a].reshape(2 * LO, C)], axis=0)
-            size = left.shape[0] // 2 if halves else left.shape[0]
-            for here in range(0, left.shape[0], size):
-                part = jnp.dot(left[here:here + size], right, preferred_element_type=F32)
-                if (k, target) in begun:
-                    part = part + sums[target - 2, here:here + size]
-                sums[target - 2, here:here + size] = part
-            begun.add((k, target))
+                left.append(sides1[f])
+        left = jnp.concatenate(left, axis=0)
+        right = []
+        for b in range(3):
+            right += [wlo[k, a, b].reshape(3 * LO, C), whi[k, a, b].reshape(LO, C)]
+        right = jnp.concatenate(right + [wti[k, a].reshape(2 * LO, C)], axis=0)
+        size = left.shape[0] // (len(frames) * pieces)
+        dots = len(frames) if pieces == 1 else pieces
+        rows = left.shape[0] // (1 if pieces == 1 else pieces)
+        made = [jnp.dot(left[i:i + rows], right, preferred_element_type=F32) for i in range(0, left.shape[0], rows)]
+        if pieces > 1:
+            return [(i * size, value) for i, value in enumerate(made)]
+        return [made[0][i * size:(i + 1) * size] for i in range(dots)]
+
+    def conv(k, a, targets, halves=False):
+        sums = (sums1, sums2)[k]
+        frames = [target - 2 + a for target in targets]
+        if halves:
+            parts = [(targets[0], here, value) for here, value in products(k, a, frames, 2)]
+        else:
+            parts = [(target, 0, value) for target, value in zip(targets, products(k, a, frames))]
+        for target, here, part in parts:
+            lines = slice(here, here + part.shape[0])
+            if (k, target) in begun:
+                part = part + sums[target - 2, lines]
+            sums[target - 2, lines] = part
+        begun.update((k, target) for target in targets)
 
     begun = set()
 
@@ -311,18 +320,18 @@
     def finish_second(frame):
         f = frame - 2
         total = sums2[f] + x[f].reshape(PX, C).astype(F32)
+        if f < 2:
+            low = late_r[f * PX:(f + 1) * PX].astype(F32)
+            high = late_r[2 * PX:3 * PX].astype(F32)[:, f * 64:(f + 1) * 64]
+            total = total + jnp.concatenate([low, high], axis=1)
         out[f] = total.astype(BF).reshape(RO, CO, C)
 
-    def pack_late(i, low, high):
-        late_s[i, 0:LINES] = low.astype(BF)
-        late_s[i, LINES:LINES + 80] = join(high[0:80], high[80:160]).astype(BF)
-        late_s[i, LINES + 80:LATE] = join(high[160:176], high[176:192]).astype(BF)
-
-    def put_late(i):
-        low = late_r[i, 0:LINES].astype(F32)
-        main = split(late_r[i, LINES:LINES + 80].astype(F32))
-        beside = split(late_r[i, LINES + 80:LATE].astype(F32))
-        put2(i, low, jnp.concatenate([*main, *beside], axis=0))
+    def pack_late():
+        last, first = products(1, 1, (5,))[0], products(1, 0, (4, 5))
+        shares = [first[0] + last, first[1]]
+        for i in range(2):
+            late_s[i * PX:(i + 1) * PX] = shares[i][:, :LO].astype(BF)
+        late_s[2 * PX:3 * PX] = jnp.concatenate([share[:, LO:] for share in shares], axis=1).astype(BF)
 
     with scope("load"):
         for load in loads:
@@ -352,44 +361,43 @@
     with scope("send_cache"):
         z_start(0)
 
+    with scope("wait_weights"):
+        for group in w_loads:
+            for load in group:
+                load.wait()
     with scope("wait_rims"):
         for side in range(8):
             rim_copy(opposite(side)).wait_recv()
         z_start(1)
-    with scope("build_own"):
+    with scope("conv_first"):
         put_rims(2)
+        build1(5)
         build1(4)
-        build1(5)
         put_rims(1)
+        build1(3)
         build1(2)
-        build1(3)
-    with scope("wait_weights"):
-        for load in w_loads[0]:
-            load.wait()
-    with scope("conv_first"):
-        conv(0, ((5, 0), (4, 0), (5, 1), (4, 1), (5, 2), (4, 2)))
-        kept = {}
+        for a in (2, 1, 0):
+            conv(0, a, (5,))
+            conv(0, a, (4,))
         for f in (5, 4):
-            kept[f] = finish_first(f)
-            pack_late(f - 4, *kept[f])
+            put2(f, *finish_first(f))
+        conv(0, 2, (2,))
+        conv(0, 2, (3,))
+        conv(0, 1, (3,), halves=True)
+        build2(5)
+        build2(4)
+        pack_late()
     with scope("send_late"):
-        z_start(3)
         z_start(2)
     with scope("conv_ahead"):
-        conv(0, ((2, 2), (3, 2)))
-        conv(0, ((3, 1),), halves=True)
-        for f in (4, 5):
-            put2(f, *kept[f])
-            build2(f)
-        for load in w_loads[1]:
-            load.wait()
-        conv(1, ((4, 2), (5, 2)))
-        conv(1, ((5, 1),), halves=True)
+        conv(1, 2, (4, 5))
+        conv(1, 1, (5,))
 
     with scope("wait_cache"):
         z_wait(0)
         z_wait(1)
-    with scope("build_cache"):
+
+    def add_cache():
         low, high = body_r[0:2 * PX].astype(F32), split(body_r[2 * PX:3 * PX].astype(F32))
         for i in range(2):
             put_body1(i, low[i * PX:(i + 1) * PX], high[i])
@@ -397,33 +405,31 @@
                 vlo[pl.ds(edge(i, 2, border), RO)] = elo1[pl.ds(at1(i, 2, border), RO, stride=EC)]
                 vhi[pl.ds(edge(i, 2, border), RO)] = ehi1[pl.ds(at1(i, 2, border), RO, stride=EC)]
         put_rims(0)
+        build1(1)
         build1(0)
-        build1(1)
-    with scope("conv_first_early"):
-        conv(0, ((2, 0), (3, 0)))
-        conv(0, ((2, 1),), halves=True)
+        conv(0, 0, (3,))
+        conv(0, 0, (2,))
+        conv(0, 1, (2,), halves=True)
+
+    with scope("cache"):
+        pl.when(has_earlier)(add_cache)
+    with scope("conv_second"):
         for f in (2, 3):
             put2(f, *finish_first(f))
+        for f in (2, 3):
             build2(f)
-    with scope("conv_second"):
-        conv(1, ((4, 0), (5, 0), (4, 1), (3, 1), (2, 2), (3, 2)))
+        conv(1, 0, (4, 5))
+        conv(1, 1, (3, 4))
+        conv(1, 2, (2,))
+        conv(1, 2, (3,))
         finish_second(4)
         finish_second(5)
 
     with scope("wait_late"):
-        z_wait(3)
-    with scope("conv_late"):
-        put_late(1)
-        build2(1)
-        conv(1, ((3, 0), (2, 1)))
+        z_wait(2)
+    with scope("finish_late"):
+        finish_second(2)
         finish_second(3)
-    with scope("wait_last"):
-        z_wait(2)
-    with scope("conv_last"):
-        put_late(0)
-        build2(0)
-        conv(1, ((2, 0),), halves=True)
-        finish_second(2)
 
     with scope("drain"):
         for side in range(8):
@@ -431,7 +437,7 @@
 
         @pl.when(has_later)
         def _():
-            for k in range(4):
+            for k in range(3):
                 z_copy(k).wait_send()
 
 
@@ -467,9 +473,9 @@
                 pltpu.VMEM((BODY, LO), BF),
                 pltpu.VMEM((2, RIM, LO), BF),
                 pltpu.VMEM((3, RIM, LO), BF),
-                pltpu.VMEM((2, LATE, LO), BF),
-                pltpu.VMEM((2, LATE, LO), BF),
-                dma((3,)), dma((2, 3)), dma((8,)), dma((8,)), dma((4,)), dma((4,)),
+                pltpu.VMEM((BODY, LO), BF),
+                pltpu.VMEM((BODY, LO), BF),
+                dma((3,)), dma((2, 3)), dma((8,)), dma((8,)), dma((3,)), dma((3,)),
             ],
             compiler_params=pltpu.CompilerParams(
                 collective_id=0, has_side_effects=True, vmem_limit_bytes=60 * 1024 * 1024),

time: 20.3 us -> 19.3 us (0.951)
  Pallas kernels: 19.5 us -> 18.5 us
    pallas_call x1, Pallas kernels: 19.5 us -> 18.5 us  [shards(): pl.pallas_call(functools.partial(kernel, sizes), out_shape=pltpu.VMEM(fea...]
where the time goes in v4:
time: 19.3 us; the launch traced here: 19.2 us
  Pallas kernels  18.5 us (96%)
  local copies, waits for them, and re-layouts  0.71 us (4%)
    pallas_call x1, Pallas kernels, shards(): pl.pallas_call(functools.partial(kernel, sizes), out_shape=pltpu.VMEM(fea...  18.5 us
    unnamed x1, local copies, waits for them, and re-layouts  0.71 us

profile of v4, /device:TPU:32, one launch (start us, length us, event | category | flops | bytes accessed | tf_op | source)
XLA Modules:
  0.0 19.2 jit_solution(13262277295941655368)
XLA Ops:
  0.0 18.5 %shard_map.55 = bf16[4,8,16,192]{3,2,1,0:T(8,128)(2,1)S(1)} custom-call(bf16[4,8,16,192]{3,2,1,0:T(8,128)(2,1)} %x_hbm.1, bf16[3,3,3,192,192]{4,3,2,1,0:T(8,128)(2,1)} %w1_hbm.1, bf16[3,3,3,192,192]{4,3,2,1,0:T(8,128)(2,1)} %w2_hbm.1, f32[1,192]{1,0:T(1,128)} %bitcast.2, f32[1,192]{1,0:T(1,128)} %bitcast.3), custom_call_target="tpu_custom_call" | custom-call | tf_op jit(solution)/shard_map/pallas_call | solution.py:450
  18.5 0.7 %copy.7 = bf16[4,8,16,192]{3,2,1,0:T(8,128)(2,1)} copy(bf16[4,8,16,192]{3,2,1,0:T(8,128)(2,1)S(1)} %shard_map.55) | data formatting | bytes 393216

commit v5 on v4

--- a/solution.py
+++ b/solution.py
@@ -361,38 +361,36 @@
     with scope("send_cache"):
         z_start(0)
 
+    with scope("wait_rims"):
+        for side in range(8):
+            rim_copy(opposite(side)).wait_recv()
+        z_start(1)
+    with scope("build_own"):
+        put_rims(1)
+        build1(3)
+        build1(2)
     with scope("wait_weights"):
         for group in w_loads:
             for load in group:
                 load.wait()
-    with scope("wait_rims"):
-        for side in range(8):
-            rim_copy(opposite(side)).wait_recv()
-        z_start(1)
     with scope("conv_first"):
+        conv(0, 0, (5,))
+        conv(0, 0, (4,))
         put_rims(2)
+        build1(4)
         build1(5)
-        build1(4)
-        put_rims(1)
-        build1(3)
-        build1(2)
-        for a in (2, 1, 0):
+        for a in (1, 2):
             conv(0, a, (5,))
             conv(0, a, (4,))
         for f in (5, 4):
             put2(f, *finish_first(f))
-        conv(0, 2, (2,))
-        conv(0, 2, (3,))
-        conv(0, 1, (3,), halves=True)
+        conv(0, 2, (2, 3))
+        conv(0, 1, (3,))
         build2(5)
         build2(4)
         pack_late()
     with scope("send_late"):
         z_start(2)
-    with scope("conv_ahead"):
-        conv(1, 2, (4, 5))
-        conv(1, 1, (5,))
-
     with scope("wait_cache"):
         z_wait(0)
         z_wait(1)
@@ -416,6 +414,8 @@
     with scope("conv_second"):
         for f in (2, 3):
             put2(f, *finish_first(f))
+        conv(1, 2, (4, 5))
+        conv(1, 1, (5,))
         for f in (2, 3):
             build2(f)
         conv(1, 0, (4, 5))

time: 19.3 us -> 19 us (0.984)
  Pallas kernels: 18.5 us -> 18.2 us
    pallas_call x1, Pallas kernels: 18.5 us -> 18.2 us  [shards(): pl.pallas_call(functools.partial(kernel, sizes), out_shape=pltpu.VMEM(fea...]
where the time goes in v5:
time: 19 us; the launch traced here: 18.9 us
  Pallas kernels  18.2 us (96%)
  local copies, waits for them, and re-layouts  0.71 us (4%)
    pallas_call x1, Pallas kernels, shards(): pl.pallas_call(functools.partial(kernel, sizes), out_shape=pltpu.VMEM(fea...  18.2 us
    unnamed x1, local copies, waits for them, and re-layouts  0.71 us

profile of v5, /device:TPU:32, one launch (start us, length us, event | category | flops | bytes accessed | tf_op | source)
XLA Modules:
  0.0 18.9 jit_solution(12697808965288677381)
XLA Ops:
  0.0 18.2 %shard_map.55 = bf16[4,8,16,192]{3,2,1,0:T(8,128)(2,1)S(1)} custom-call(bf16[4,8,16,192]{3,2,1,0:T(8,128)(2,1)} %x_hbm.1, bf16[3,3,3,192,192]{4,3,2,1,0:T(8,128)(2,1)} %w1_hbm.1, bf16[3,3,3,192,192]{4,3,2,1,0:T(8,128)(2,1)} %w2_hbm.1, f32[1,192]{1,0:T(1,128)} %bitcast.2, f32[1,192]{1,0:T(1,128)} %bitcast.3), custom_call_target="tpu_custom_call" | custom-call | tf_op jit(solution)/shard_map/pallas_call | solution.py:450
  18.2 0.7 %copy.7 = bf16[4,8,16,192]{3,2,1,0:T(8,128)(2,1)} copy(bf16[4,8,16,192]{3,2,1,0:T(8,128)(2,1)S(1)} %shard_map.55) | data formatting | bytes 393216

commit v6 on v5

--- a/solution.py
+++ b/solution.py
@@ -89,9 +89,16 @@
     has_later = tm < n_tm - 1
     has_earlier = tm > 0
 
+    up, down, left, right = row > 0, row < n_row - 1, col > 0, col < n_col - 1
+    beside = (
+        up, down, left, right, jnp.logical_and(up, left), jnp.logical_and(up, right),
+        jnp.logical_and(down, left), jnp.logical_and(down, right))
+
     barrier = pltpu.get_barrier_semaphore()
-    for dr, dc in SIDES:
-        pl.semaphore_signal(barrier, inc=1, device_id=neighbour(dr, dc), device_id_type=MESH)
+    for side, (dr, dc) in enumerate(SIDES):
+        @pl.when(beside[side])
+        def _():
+            pl.semaphore_signal(barrier, inc=1, device_id=neighbour(dr, dc), device_id_type=MESH)
 
     @pl.when(has_earlier)
     def _():
@@ -122,11 +129,12 @@
     keep_row = {-1: jnp.where(row > 0, 1.0, 0.0), 1: jnp.where(row < n_row - 1, 1.0, 0.0)}
     keep_col = {-1: jnp.where(col > 0, 1.0, 0.0), 1: jnp.where(col < n_col - 1, 1.0, 0.0)}
 
-    def side_keep(side):
-        dr, dc = SIDES[side]
-        if dr and dc:
-            return keep_row[dr] * keep_col[dc]
-        return keep_row[dr] if dr else keep_col[dc]
+    for side in range(8):
+        here, size = SPOT[side]
+
+        @pl.when(jnp.logical_not(beside[side]))
+        def _():
+            rim_r[1:3, here:here + size] = jnp.zeros((2, size, LO), BF)
 
     def rim_copy(side):
         here, size = SPOT[side]
@@ -197,7 +205,7 @@
             spot, size = SPOT[side]
             r = 0 if dr < 0 else RO + 2
             c = 6 if dc < 0 else 24
-            value = rim_r[slot, spot:spot + size].astype(F32) * side_keep(side)
+            value = rim_r[slot, spot:spot + size].astype(F32)
             near = 1 if dc < 0 else 0
             for i in range(2):
                 for q in range(2):
@@ -354,16 +362,19 @@
         body_s[2 * PX:3 * PX] = join(kept[2][1], kept[3][1]).astype(BF)
 
     with scope("barrier"):
-        pl.semaphore_wait(barrier, jnp.where(has_later, 9, 8))
+        count = jnp.where(has_later, 1, 0)
+        for side in range(8):
+            count = count + jnp.where(beside[side], 1, 0)
+        pl.semaphore_wait(barrier, count)
     with scope("send_rims"):
         for side in reversed(range(8)):
-            rim_copy(side).start()
+            pl.when(beside[side])(lambda: rim_copy(side).start())
     with scope("send_cache"):
         z_start(0)
 
     with scope("wait_rims"):
         for side in range(8):
-            rim_copy(opposite(side)).wait_recv()
+            pl.when(beside[side])(lambda: rim_copy(opposite(side)).wait_recv())
         z_start(1)
     with scope("build_own"):
         put_rims(1)
@@ -433,7 +444,7 @@
 
     with scope("drain"):
         for side in range(8):
-            rim_copy(side).wait_send()
+            pl.when(beside[side])(lambda: rim_copy(side).wait_send())
 
         @pl.when(has_later)
         def _():

time: 19 us -> 16.9 us (0.89)
  Pallas kernels: 18.2 us -> 16.1 us
    pallas_call x1, Pallas kernels: 18.2 us -> 16.1 us  [shards(): pl.pallas_call(functools.partial(kernel, sizes), out_shape=pltpu.VMEM(fea...]
where the time goes in v6:
time: 16.9 us; the launch traced here: 16.8 us
  Pallas kernels  16.1 us (95%)
  local copies, waits for them, and re-layouts  0.71 us (4%)
    pallas_call x1, Pallas kernels, shards(): pl.pallas_call(functools.partial(kernel, sizes), out_shape=pltpu.VMEM(fea...  16.1 us
    unnamed x1, local copies, waits for them, and re-layouts  0.71 us

profile of v6, /device:TPU:32, one launch (start us, length us, event | category | flops | bytes accessed | tf_op | source)
XLA Modules:
  0.0 16.8 jit_solution(9411890731195645820)
XLA Ops:
  0.0 16.1 %shard_map.55 = bf16[4,8,16,192]{3,2,1,0:T(8,128)(2,1)S(1)} custom-call(bf16[4,8,16,192]{3,2,1,0:T(8,128)(2,1)} %x_hbm.1, bf16[3,3,3,192,192]{4,3,2,1,0:T(8,128)(2,1)} %w1_hbm.1, bf16[3,3,3,192,192]{4,3,2,1,0:T(8,128)(2,1)} %w2_hbm.1, f32[1,192]{1,0:T(1,128)} %bitcast.2, f32[1,192]{1,0:T(1,128)} %bitcast.3), custom_call_target="tpu_custom_call" | custom-call | tf_op jit(solution)/shard_map/pallas_call | solution.py:461
  16.1 0.7 %copy.7 = bf16[4,8,16,192]{3,2,1,0:T(8,128)(2,1)} copy(bf16[4,8,16,192]{3,2,1,0:T(8,128)(2,1)S(1)} %shard_map.55) | data formatting | bytes 393216

commit v7 on v6

--- a/solution.py
+++ b/solution.py
@@ -473,8 +473,8 @@
                 pltpu.VMEM((EF * ER1 * EC, LO), F32),
                 pltpu.VMEM((EF * len(EDGE) * EL, LO), F32),
                 pltpu.VMEM((EF * len(EDGE) * EL, LO), F32),
-                pltpu.VMEM((EF * ER2 * EC, LO), F32),
-                pltpu.VMEM((EF * ER2 * EC, LO), F32),
+                pltpu.VMEM(((EF + 1) * ER2 * EC, LO), F32),
+                pltpu.VMEM(((EF + 1) * ER2 * EC, LO), F32),
                 pltpu.VMEM((EF, ER1 * CO, 5 * LO), BF),
                 pltpu.VMEM((EF, SIDE, 14 * LO), BF),
                 pltpu.VMEM((EF, ER2 * CO, 5 * LO), BF),

time: 16.9 us -> 16.9 us (level)
  no operation moved by 1% of the time
where the time goes in v7:
time: 16.9 us; the launch traced here: 16.8 us
  Pallas kernels  16.1 us (95%)
  local copies, waits for them, and re-layouts  0.71 us (4%)
    pallas_call x1, Pallas kernels, shards(): pl.pallas_call(functools.partial(kernel, sizes), out_shape=pltpu.VMEM(fea...  16.1 us
    unnamed x1, local copies, waits for them, and re-layouts  0.71 us

profile of v7, /device:TPU:32, one launch (start us, length us, event | category | flops | bytes accessed | tf_op | source)
XLA Modules:
  0.0 16.8 jit_solution(963995118525866156)
XLA Ops:
  0.0 16.1 %shard_map.55 = bf16[4,8,16,192]{3,2,1,0:T(8,128)(2,1)S(1)} custom-call(bf16[4,8,16,192]{3,2,1,0:T(8,128)(2,1)} %x_hbm.1, bf16[3,3,3,192,192]{4,3,2,1,0:T(8,128)(2,1)} %w1_hbm.1, bf16[3,3,3,192,192]{4,3,2,1,0:T(8,128)(2,1)} %w2_hbm.1, f32[1,192]{1,0:T(1,128)} %bitcast.2, f32[1,192]{1,0:T(1,128)} %bitcast.3), custom_call_target="tpu_custom_call" | custom-call | tf_op jit(solution)/shard_map/pallas_call | solution.py:461
  16.1 0.7 %copy.7 = bf16[4,8,16,192]{3,2,1,0:T(8,128)(2,1)} copy(bf16[4,8,16,192]{3,2,1,0:T(8,128)(2,1)S(1)} %shard_map.55) | data formatting | bytes 393216
